TPU v7x, 512 devices: a whole 4x4x16 slice. The times are simulated.
512 devices in a mesh: grp: 8 (over x_hi, y), seq: 64 (over z, x_lo, core).
Axes of the slice: x: 4 (x_hi: 2, x_lo: 2; x = x_hi * 2 + x_lo), y: 4, z: 16, core: 2. Of those that a mesh axis runs over, the one named last changes fastest.
Arguments:
- queries: bfloat16 [65536, 4096], P(('grp', 'seq')), parts along dimension 0, may hold values from -6.5 to 6.5
- resp_key: bfloat16 [65536, 512], P(('grp', 'seq')), parts along dimension 0, may hold values from -6 to 6
- resp_value: bfloat16 [65536, 512], P(('grp', 'seq')), parts along dimension 0, may hold values from -12 to 12
- prompt_key: bfloat16 [4096, 512], P(('grp', 'seq')), parts along dimension 0, may hold values from -6 to 6
- prompt_value: bfloat16 [4096, 512], P(('grp', 'seq')), parts along dimension 0, may hold values from -12 to 12
- out_grad: bfloat16 [65536, 4096], P(('grp', 'seq')), parts along dimension 0, may hold values from -24 to 24
- segment: int32 [65536], P(('grp', 'seq')), parts along dimension 0, may hold values from 0 to 31, never falling along the last dimension, each value on 1 to 385 neighbouring positions
Outputs:
- query_grad: bfloat16 [65536, 4096], P(('grp', 'seq')), parts along dimension 0
- resp_key_grad: float32 [65536, 512], P(('grp', 'seq')), parts along dimension 0
- resp_value_grad: float32 [65536, 512], P(('grp', 'seq')), parts along dimension 0
- prompt_key_grad: float32 [4096, 512], P(('grp', 'seq')), parts along dimension 0
- prompt_value_grad: float32 [4096, 512], P(('grp', 'seq')), parts along dimension 0
There are 8 independent parts, one for each index of `grp`. A program takes and returns all parts, laid end to end along the dimension named above; each array names one. Nothing has to cross between parts.
Inputs may be any that keep to these rules, and one draw needn't show every extreme that they name: segment numbers never fall along the rows; every response holds 1 to 385 tokens, one exactly 385.
All inputs are finite; a program needn't handle non-finite values.
Results may differ from a plain program's by a relative error of at most 0.0059.
Values may be sent and summed in bfloat16 or wider, within the bound.
A program may use at most 64 MiB of HBM per device.

v0:
```python
import jax
import jax.numpy as jnp
from jax import lax
from jax.sharding import PartitionSpec as P

HQ = 32
HK = 4
HD = 128
BACK = 3


def passed_along(value, axis, by):
    count = lax.axis_size(axis)
    pairs = [(i, i + by) for i in range(count) if 0 <= i + by < count]
    return lax.ppermute(value, axis, pairs)


def head_terms(head_queries, head_grads, head_keys, head_values, allowed, scaling, prompt_total):
    scores = (
        jnp.einsum("rgd,nd->grn", head_queries, head_keys, preferred_element_type=jnp.float32)
        * scaling
    )
    scores = jnp.where(allowed[None], scores, -jnp.inf)
    highest = jnp.max(scores, axis=2, keepdims=True)
    log_total = highest + jnp.log(jnp.sum(jnp.exp(scores - highest), axis=2, keepdims=True))
    weights = jnp.exp(scores - log_total)
    rounded = weights.astype(jnp.bfloat16)
    outputs = jnp.einsum("grn,nd->rgd", rounded, head_values, preferred_element_type=jnp.float32)
    row_delta = jnp.sum(head_grads.astype(jnp.float32) * outputs, axis=2)
    weight_grads = jnp.einsum(
        "rgd,nd->grn", head_grads, head_values, preferred_element_type=jnp.float32
    )
    score_grads = (
        weights * (weight_grads - jnp.transpose(row_delta)[:, :, None]) * scaling
    ).astype(jnp.bfloat16)
    grad_query = jnp.einsum(
        "grn,nd->rgd", score_grads, head_keys, preferred_element_type=jnp.float32
    )
    grad_keys = jnp.einsum(
        "grn,rgd->nd",
        score_grads[:, :, prompt_total:],
        head_queries,
        preferred_element_type=jnp.float32,
    )
    grad_values = jnp.einsum(
        "grn,rgd->nd", rounded[:, :, prompt_total:], head_grads, preferred_element_type=jnp.float32
    )
    return (
        grad_query,
        grad_keys,
        grad_values,
        score_grads[:, :, :prompt_total],
        rounded[:, :, :prompt_total],
    )


def attend_block(queries, out_grad, all_keys, all_values, allowed, prompt_total):
    row_count = queries.shape[0]
    group_size = HQ // HK
    scaling = HD ** (-0.5)
    grad_query, grad_keys, grad_values, score_parts, weight_parts = ([], [], [], [], [])
    for head_index in range(HK):
        col_lower = head_index * group_size * HD
        col_upper = col_lower + group_size * HD
        head_queries = queries[:, col_lower:col_upper].reshape(row_count, group_size, HD)
        head_grads = out_grad[:, col_lower:col_upper].reshape(row_count, group_size, HD)
        head_keys = all_keys[:, head_index * HD : (head_index + 1) * HD]
        head_values = all_values[:, head_index * HD : (head_index + 1) * HD]
        results = head_terms(
            head_queries, head_grads, head_keys, head_values, allowed, scaling, prompt_total
        )
        grad_query.append(results[0].reshape(row_count, group_size * HD))
        grad_keys.append(results[1])
        grad_values.append(results[2])
        score_parts.append(results[3])
        weight_parts.append(results[4])
    return (
        jnp.concatenate(grad_query, axis=1),
        jnp.concatenate(grad_keys, axis=1),
        jnp.concatenate(grad_values, axis=1),
        jnp.stack(score_parts),
        jnp.stack(weight_parts),
    )


def prompt_term(score_stack, weight_stack, query_heads, grad_heads, row_span):
    key_terms = jnp.einsum(
        "kgrn,rkgd->nkd", score_stack, query_heads, preferred_element_type=jnp.float32
    )
    value_terms = jnp.einsum(
        "kgrn,rkgd->nkd", weight_stack, grad_heads, preferred_element_type=jnp.float32
    )
    return jnp.concatenate(
        (key_terms.reshape(row_span, HK * HD), value_terms.reshape(row_span, HK * HD)), axis=1
    )


def on_device(queries, resp_key, resp_value, prompt_key, prompt_value, out_grad, segment):
    row_count = queries.shape[0]
    block_rows = prompt_key.shape[0]
    kv_width = prompt_key.shape[1]
    group_size = HQ // HK
    prompt_keys, prompt_values = (
        lax.all_gather(prompt_key, "seq", axis=0, tiled=True),
        lax.all_gather(prompt_value, "seq", axis=0, tiled=True),
    )
    prompt_total = prompt_keys.shape[0]
    own_labels = segment + 1
    own_pair = jnp.stack((resp_key, resp_value))
    earlier = []
    earlier_labels = []
    for offset in range(1, BACK + 1):
        pair_here, labels_here = passed_along((own_pair, own_labels), "seq", offset)
        earlier.append(pair_here)
        earlier_labels.append(labels_here)
    row_index = lax.broadcasted_iota(jnp.int32, (row_count, row_count), 0)
    col_index = lax.broadcasted_iota(jnp.int32, (row_count, row_count), 1)
    masks = [jnp.ones((row_count, prompt_total), jnp.bool_)]
    key_parts = [prompt_keys]
    value_parts = [prompt_values]
    for offset in range(BACK, 0, -1):
        masks.append(own_labels[:, None] == earlier_labels[offset - 1][None, :])
        key_parts.append(earlier[offset - 1][0])
        value_parts.append(earlier[offset - 1][1])
    masks.append((own_labels[:, None] == own_labels[None, :]) & (col_index <= row_index))
    key_parts.append(resp_key)
    value_parts.append(resp_value)
    allowed = jnp.concatenate(masks, axis=1)
    all_keys = jnp.concatenate(key_parts, axis=0)
    all_values = jnp.concatenate(value_parts, axis=0)
    grad_query, tail_keys, tail_values, score_stack, weight_stack = attend_block(
        queries, out_grad, all_keys, all_values, allowed, prompt_total
    )

    def slot_pair(offset):
        lower = (BACK - offset) * row_count
        return jnp.stack(
            (tail_keys[lower : lower + row_count], tail_values[lower : lower + row_count])
        )

    returned = jnp.zeros((2, row_count, kv_width), jnp.float32)
    for offset in range(1, BACK + 1):
        returned = returned + passed_along(
            slot_pair(offset).astype(jnp.bfloat16), "seq", -offset
        ).astype(jnp.float32)
    own_slot = slot_pair(0)
    key_grad = own_slot[0] + returned[0]
    value_grad = own_slot[1] + returned[1]
    query_heads = queries.reshape(row_count, HK, group_size, HD)
    grad_heads = out_grad.reshape(row_count, HK, group_size, HD)
    prompt_sum = lax.psum_scatter(
        prompt_term(
            score_stack, weight_stack, query_heads, grad_heads, block_rows * lax.axis_size("seq")
        ),
        "seq",
        scatter_dimension=0,
        tiled=True,
    )
    return (
        grad_query.astype(jnp.bfloat16),
        key_grad,
        value_grad,
        prompt_sum[:, :kv_width],
        prompt_sum[:, kv_width:],
    )


def solution(mesh):
    return jax.shard_map(
        on_device,
        mesh=mesh,
        in_specs=(
            P(("grp", "seq"), None),
            P(("grp", "seq"), None),
            P(("grp", "seq"), None),
            P(("grp", "seq"), None),
            P(("grp", "seq"), None),
            P(("grp", "seq"), None),
            P(("grp", "seq")),
        ),
        out_specs=(
            P(("grp", "seq"), None),
            P(("grp", "seq"), None),
            P(("grp", "seq"), None),
            P(("grp", "seq"), None),
            P(("grp", "seq"), None),
        ),
        check_vma=False,
    )
```

profile of v0, /device:TPU:24, one launch (start us, length us, event | category | flops | bytes accessed | tf_op | source)
XLA Modules:
  0.0 457.4 jit_solution(12606021987235708357)
XLA Ops:
  8.0 1.7 collective-permute-start.5
  9.7 3.6 collective-permute-start.4
  13.3 4.7 %collective-permute-start.3 = (s32[128]{0:T(128)S(1)}, s32[128]{0:T(128)S(1)}, u32[]{:S(2)}, u32[]{:S(2)}) collective-permute-start(s32[128]{0:T(128)S(1)} %broadcast_add_fusion), channel_id=1, source_target_pairs={{0,3},{1,4},{2,5},{3,6},{4,7},{5,8},{6,9},{7,10},{8,11},{9,12},{10... | collective-permute-start | bytes 1544 | tf_op jit(solution)/shard_map/ppermute | solution.py:15
  18.0 1.7 pad_maximum_fusion.4
  19.7 2.0 collective-permute-start.2
  21.7 4.4 collective-permute-start.1
  26.1 68.1 %all_gather.6 = bf16[512,512]{1,0:T(8,128)(2,1)S(1)} all-gather(bf16[8,512]{1,0:T(8,128)(2,1)} %param.10), channel_id=1, replica_groups=mesh['grp'=8,'seq'=64] {'seq'}, dimensions={0}, use_global_device_ids=true | all-gather | bytes 532480 | tf_op jit(solution)/shard_map/all_gather | solution.py:104
  94.3 61.6 %all_gather.7 = bf16[512,512]{1,0:T(8,128)(2,1)S(1)} all-gather(bf16[8,512]{1,0:T(8,128)(2,1)} %param.11), channel_id=1, replica_groups=mesh['grp'=8,'seq'=64] {'seq'}, dimensions={0}, use_global_device_ids=true | all-gather | bytes 532480 | tf_op jit(solution)/shard_map/all_gather | solution.py:105
  157.4 2.0 copy.62
  159.5 0.9 fusion.70
  160.5 3.2 collective-permute-start
  164.1 3.8 collective-permute-done
  168.5 1.6 fusion.59
  170.2 1.6 fusion.58
  174.7 2.6 exponential_reduce_fusion.3
  177.3 2.8 exponential_reduce_fusion.2
  180.1 3.7 fusion.28
  183.9 2.1 fusion.40
  186.1 1.5 fusion.18
  188.1 1.2 slice_bitcast_fusion.4
  189.9 1.5 fusion.21
  191.4 1.4 convolution_convert_fusion.1
  192.9 1.0 slice_bitcast_fusion.5
  194.5 2.8 fusion.27
  197.9 2.8 fusion.24
  200.7 2.4 fusion.8
  203.1 2.5 copy.109
  205.7 1.4 slice_bitcast_fusion.6
  207.1 1.3 slice_bitcast_fusion.7
  208.5 2.4 fusion
  210.9 2.6 copy.108
  213.4 3.1 pad_maximum_fusion
  216.6 2.8 convolution_convert_fusion.3
  219.3 0.8 copy.95
  220.2 1.8 copy.94
  222.0 1.8 copy.92
  223.8 2.1 convolution_convert_fusion.2
  226.0 1.9 convolution_bitcast_fusion.11
  227.9 1.9 convolution_bitcast_fusion.10
  229.9 1.9 convolution_bitcast_fusion.9
  234.6 1.3 collective-permute-start.7
  236.0 1.3 collective-permute-start.8
  237.3 1.3 collective-permute-start.6
  238.6 1.0 pad_maximum_fusion.1
  239.8 6.7 %collective-permute-done.7 = bf16[2,128,512]{1,2,0:T(8,128)(2,1)S(1)} collective-permute-done((bf16[2,128,512]{1,2,0:T(8,128)(2,1)S(1)}, bf16[2,128,512]{1,2,0:T(8,128)(2,1)S(1)}, u32[]{:S(2)}, u32[]{:S(2)}) %collective-permute-start.7) | collective-permute-done | bytes 262176 | tf_op jit(solution)/shard_map/ppermute | solution.py:15
  246.5 5.3 %collective-permute-done.8 = bf16[2,128,512]{1,2,0:T(8,128)(2,1)S(1)} collective-permute-done((bf16[2,128,512]{1,2,0:T(8,128)(2,1)S(1)}, bf16[2,128,512]{1,2,0:T(8,128)(2,1)S(1)}, u32[]{:S(2)}, u32[]{:S(2)}) %collective-permute-start.8) | collective-permute-done | bytes 262176 | tf_op jit(solution)/shard_map/ppermute | solution.py:15
  253.7 195.5 %reduce-scatter.2.cloned.1.call-done = f32[8,1024]{1,0:T(8,128)} async-done(((f32[512,1024]{1,0:T(8,128)}), f32[8,1024]{1,0:T(8,128)}) %reduce-scatter.2.cloned.1.call-update) | async-done | bytes 32784 | tf_op jit(solution)/shard_map/reduce_scatter | solution.py:151
  449.2 1.3 fusion.72
  (123 shorter events, 13.6 us)
Async XLA Ops:
  7.2 149.6 %copy-start.14 = (bf16[128,4096]{1,0:T(8,128)(2,1)S(1)}, bf16[128,4096]{1,0:T(8,128)(2,1)}, u32[]{:S(2)}) copy-start(bf16[128,4096]{1,0:T(8,128)(2,1)} %param.7) | copy-start | bytes 3145732
  7.2 442.1 %reduce-scatter.2.cloned.1.call-start = ((), (), s32[]{:S(2)}) async-start(), calls=%async_computation.1 | async-start | bytes 2129920 | tf_op jit(solution)/shard_map/reduce_scatter | solution.py:151
  8.0 155.9 %collective-permute-start.5 = (s32[128]{0:T(128)S(1)}, s32[128]{0:T(128)S(1)}, u32[]{:S(2)}, u32[]{:S(2)}) collective-permute-start(s32[128]{0:T(128)S(1)} %broadcast_add_fusion), channel_id=1, source_target_pairs={{0,1},{1,2},{2,3},{3,4},{4,5},{5,6},{6,7},{7,8},{8,9},{9,10},{10,1... | collective-permute-start | bytes 1544 | tf_op jit(solution)/shard_map/ppermute | solution.py:15
  9.7 154.1 %collective-permute-start.4 = (s32[128]{0:T(128)S(1)}, s32[128]{0:T(128)S(1)}, u32[]{:S(2)}, u32[]{:S(2)}) collective-permute-start(s32[128]{0:T(128)S(1)} %broadcast_add_fusion), channel_id=1, source_target_pairs={{0,2},{1,3},{2,4},{3,5},{4,6},{5,7},{6,8},{7,9},{8,10},{9,11},{10,... | collective-permute-start | bytes 1544 | tf_op jit(solution)/shard_map/ppermute | solution.py:15
  13.3 147.2 %collective-permute-start.3 = (s32[128]{0:T(128)S(1)}, s32[128]{0:T(128)S(1)}, u32[]{:S(2)}, u32[]{:S(2)}) collective-permute-start(s32[128]{0:T(128)S(1)} %broadcast_add_fusion), channel_id=1, source_target_pairs={{0,3},{1,4},{2,5},{3,6},{4,7},{5,8},{6,9},{7,10},{8,11},{9,12},{10... | collective-permute-start | bytes 1544 | tf_op jit(solution)/shard_map/ppermute | solution.py:15
  19.7 150.5 %collective-permute-start.2 = (bf16[2,128,512]{2,1,0:T(8,128)(2,1)}, bf16[2,128,512]{2,1,0:T(8,128)(2,1)}, u32[]{:S(2)}, u32[]{:S(2)}) collective-permute-start(bf16[2,128,512]{2,1,0:T(8,128)(2,1)} %pad_maximum_fusion.4), channel_id=1, source_target_pairs={{0,1},{1,2},{2,3},{3,4},{4,5},{5,6},{6,7},{7,8},{8,9},{9,10},{10,1... | collective-permute-start | bytes 786440 | tf_op jit(solution)/shard_map/ppermute | solution.py:15
  21.7 146.8 %collective-permute-start.1 = (bf16[2,128,512]{2,1,0:T(8,128)(2,1)}, bf16[2,128,512]{2,1,0:T(8,128)(2,1)}, u32[]{:S(2)}, u32[]{:S(2)}) collective-permute-start(bf16[2,128,512]{2,1,0:T(8,128)(2,1)} %pad_maximum_fusion.4), channel_id=1, source_target_pairs={{0,2},{1,3},{2,4},{3,5},{4,6},{5,7},{6,8},{7,9},{8,10},{9,11},{10,... | collective-permute-start | bytes 786440 | tf_op jit(solution)/shard_map/ppermute | solution.py:15
  157.4 15.1 %copy-start.9 = (bf16[128,4096]{0,1:T(8,128)(2,1)}, bf16[128,4096]{0,1:T(8,128)(2,1)S(1)}, u32[]{:S(2)}) copy-start(bf16[128,4096]{0,1:T(8,128)(2,1)S(1)} %copy.60) | copy-start | bytes 3145732
  157.4 14.4 %copy-start.32 = (bf16[128,512]{1,0:T(8,128)(2,1)S(1)}, bf16[128,512]{1,0:T(8,128)(2,1)}, u32[]{:S(2)}) copy-start(bf16[128,512]{1,0:T(8,128)(2,1)} %param.9) | copy-start | bytes 393220
  159.5 13.7 %copy-start.11 = (bf16[128,4096]{0,1:T(8,128)(2,1)}, bf16[128,4096]{0,1:T(8,128)(2,1)S(1)}, u32[]{:S(2)}) copy-start(bf16[128,4096]{0,1:T(8,128)(2,1)S(1)} %copy.62) | copy-start | bytes 3145732
  159.5 13.0 %copy-start.33 = (bf16[128,512]{1,0:T(8,128)(2,1)S(1)}, bf16[128,512]{1,0:T(8,128)(2,1)}, u32[]{:S(2)}) copy-start(bf16[128,512]{1,0:T(8,128)(2,1)} %param.8) | copy-start | bytes 393220
  160.4 25.6 %copy-start.17 = (bf16[128,1024]{0,1:T(8,128)(2,1)}, bf16[128,1024]{0,1:T(8,128)(2,1)S(1)}, u32[]{:S(2)}) copy-start(bf16[128,1024]{0,1:T(8,128)(2,1)S(1)} %get-tuple-element.23) | copy-start | bytes 786436
  160.4 13.5 %copy-start.25 = (bf16[128,1024]{0,1:T(8,128)(2,1)}, bf16[128,1024]{0,1:T(8,128)(2,1)S(1)}, u32[]{:S(2)}) copy-start(bf16[128,1024]{0,1:T(8,128)(2,1)S(1)} %get-tuple-element.27) | copy-start | bytes 786436
  160.4 13.5 %copy-start.27 = (bf16[128,1024]{0,1:T(8,128)(2,1)}, bf16[128,1024]{0,1:T(8,128)(2,1)S(1)}, u32[]{:S(2)}) copy-start(bf16[128,1024]{0,1:T(8,128)(2,1)S(1)} %get-tuple-element.26) | copy-start | bytes 786436
  160.5 13.5 %copy-start.28 = (bf16[128,1024]{0,1:T(8,128)(2,1)}, bf16[128,1024]{0,1:T(8,128)(2,1)S(1)}, u32[]{:S(2)}) copy-start(bf16[128,1024]{0,1:T(8,128)(2,1)S(1)} %get-tuple-element.29) | copy-start | bytes 786436
  160.5 14.2 %copy-start.34 = (bf16[128,1024]{0,1:T(8,128)(2,1)}, bf16[128,1024]{0,1:T(8,128)(2,1)S(1)}, u32[]{:S(2)}) copy-start(bf16[128,1024]{0,1:T(8,128)(2,1)S(1)} %get-tuple-element.28) | copy-start | bytes 786436
  160.5 7.3 %collective-permute-start = (bf16[2,128,512]{2,1,0:T(8,128)(2,1)}, bf16[2,128,512]{2,1,0:T(8,128)(2,1)S(1)}, u32[]{:S(2)}, u32[]{:S(2)}) collective-permute-start(bf16[2,128,512]{2,1,0:T(8,128)(2,1)} %pad_maximum_fusion.4), channel_id=1, source_target_pairs={{0,3},{1,4},{2,5},{3,6},{4,7},{5,8},{6,9},{7,10},{8,11},{9,12},{10... | collective-permute-start | bytes 786440 | tf_op jit(solution)/shard_map/ppermute | solution.py:15
  183.8 5.6 %copy-start = (bf16[8,128,1024]{1,2,0:T(8,128)(2,1)}, bf16[8,128,1024]{1,2,0:T(8,128)(2,1)S(1)}, u32[]{:S(2)}) copy-start(bf16[8,128,1024]{1,2,0:T(8,128)(2,1)S(1)} %get-tuple-element.46) | copy-start | bytes 6291460
  183.8 10.2 %copy-start.4 = (bf16[8,128,1024]{1,2,0:T(8,128)(2,1)}, bf16[8,128,1024]{1,2,0:T(8,128)(2,1)S(1)}, u32[]{:S(2)}) copy-start(bf16[8,128,1024]{1,2,0:T(8,128)(2,1)S(1)} %get-tuple-element.44) | copy-start | bytes 6291460
  183.8 13.6 %copy-start.2 = (bf16[8,128,1024]{1,2,0:T(8,128)(2,1)}, bf16[8,128,1024]{1,2,0:T(8,128)(2,1)S(1)}, u32[]{:S(2)}) copy-start(bf16[8,128,1024]{1,2,0:T(8,128)(2,1)S(1)} %get-tuple-element.45) | copy-start | bytes 6291460
  183.8 2.3 copy-start.13
  187.6 2.3 copy-start.6
  187.6 1.7 copy-start.19
  191.4 3.1 copy-start.8
  191.4 2.6 copy-start.23
  194.5 2.9 copy-start.21
  197.9 2.8 copy-start.12
  205.7 2.8 copy-start.10
  205.7 2.8 copy-start.15
  205.7 2.8 copy-start.16
  225.8 5.9 %copy-start.26 = (bf16[128,1024]{0,1:T(8,128)(2,1)S(1)}, bf16[128,1024]{0,1:T(8,128)(2,1)}, u32[]{:S(2)}) copy-start(bf16[128,1024]{0,1:T(8,128)(2,1)} %copy-done.25) | copy-start | bytes 786436
  226.0 5.8 %copy-start.7 = (bf16[8,128,1024]{1,2,0:T(8,128)(2,1)S(1)}, bf16[8,128,1024]{1,2,0:T(8,128)(2,1)}, u32[]{:S(2)}) copy-start(bf16[8,128,1024]{1,2,0:T(8,128)(2,1)} %copy-done.6) | copy-start | bytes 6291460
  226.0 6.3 %copy-start.5 = (bf16[8,128,1024]{1,2,0:T(8,128)(2,1)S(1)}, bf16[8,128,1024]{1,2,0:T(8,128)(2,1)}, u32[]{:S(2)}) copy-start(bf16[8,128,1024]{1,2,0:T(8,128)(2,1)} %copy-done.4) | copy-start | bytes 6291460
  226.0 6.3 %copy-start.24 = (bf16[128,1024]{0,1:T(8,128)(2,1)S(1)}, bf16[128,1024]{0,1:T(8,128)(2,1)}, u32[]{:S(2)}) copy-start(bf16[128,1024]{0,1:T(8,128)(2,1)} %get-tuple-element.22) | copy-start | bytes 786436
  227.9 4.9 %copy-start.3 = (bf16[8,128,1024]{1,2,0:T(8,128)(2,1)S(1)}, bf16[8,128,1024]{1,2,0:T(8,128)(2,1)}, u32[]{:S(2)}) copy-start(bf16[8,128,1024]{1,2,0:T(8,128)(2,1)} %copy-done.2) | copy-start | bytes 6291460
  227.9 4.9 %copy-start.22 = (bf16[128,1024]{0,1:T(8,128)(2,1)S(1)}, bf16[128,1024]{0,1:T(8,128)(2,1)}, u32[]{:S(2)}) copy-start(bf16[128,1024]{0,1:T(8,128)(2,1)} %get-tuple-element.25) | copy-start | bytes 786436
  229.8 3.5 copy-start.1
  229.9 3.5 copy-start.20
  231.8 2.1 copy-start.18
  233.4 5.2 %copy-start.29 = (bf16[128,1024]{1,0:T(8,128)(2,1)S(1)}, bf16[128,1024]{1,0:T(8,128)(2,1)}, u32[]{:S(2)}) copy-start(bf16[128,1024]{1,0:T(8,128)(2,1)} %copy.95) | copy-start | bytes 786436
  233.4 5.2 %copy-start.30 = (bf16[128,1024]{1,0:T(8,128)(2,1)S(1)}, bf16[128,1024]{1,0:T(8,128)(2,1)}, u32[]{:S(2)}) copy-start(bf16[128,1024]{1,0:T(8,128)(2,1)} %copy.94) | copy-start | bytes 786436
  233.4 5.2 %copy-start.31 = (bf16[128,1024]{1,0:T(8,128)(2,1)S(1)}, bf16[128,1024]{1,0:T(8,128)(2,1)}, u32[]{:S(2)}) copy-start(bf16[128,1024]{1,0:T(8,128)(2,1)} %copy.92) | copy-start | bytes 786436
  234.6 11.9 %collective-permute-start.7 = (bf16[2,128,512]{1,2,0:T(8,128)(2,1)S(1)}, bf16[2,128,512]{1,2,0:T(8,128)(2,1)S(1)}, u32[]{:S(2)}, u32[]{:S(2)}) collective-permute-start(bf16[2,128,512]{1,2,0:T(8,128)(2,1)S(1)} %pad_maximum_fusion.6), channel_id=1, source_target_pairs={{2,0},{3,1},{4,2},{5,3},{6,4},{7,5},{8,6},{9,7},{10,8},{11,9},{12,... | collective-permute-start | bytes 786440 | tf_op jit(solution)/shard_map/ppermute | solution.py:15
  236.0 15.9 %collective-permute-start.8 = (bf16[2,128,512]{1,2,0:T(8,128)(2,1)S(1)}, bf16[2,128,512]{1,2,0:T(8,128)(2,1)S(1)}, u32[]{:S(2)}, u32[]{:S(2)}) collective-permute-start(bf16[2,128,512]{1,2,0:T(8,128)(2,1)S(1)} %pad_maximum_fusion.7), channel_id=1, source_target_pairs={{3,0},{4,1},{5,2},{6,3},{7,4},{8,5},{9,6},{10,7},{11,8},{12,9},{13... | collective-permute-start | bytes 786440 | tf_op jit(solution)/shard_map/ppermute | solution.py:15
  237.3 14.6 %collective-permute-start.6 = (bf16[2,128,512]{1,2,0:T(8,128)(2,1)S(1)}, bf16[2,128,512]{1,2,0:T(8,128)(2,1)S(1)}, u32[]{:S(2)}, u32[]{:S(2)}) collective-permute-start(bf16[2,128,512]{1,2,0:T(8,128)(2,1)S(1)} %pad_maximum_fusion.5), channel_id=1, source_target_pairs={{1,0},{2,1},{3,2},{4,3},{5,4},{6,5},{7,6},{8,7},{9,8},{10,9},{11,1... | collective-permute-start | bytes 786440 | tf_op jit(solution)/shard_map/ppermute | solution.py:15
Sparse Core Ops, SparseCore 0:
  216.7 232.4 reduce-scatter.1
where the time goes:
time: 458 us; the launch traced here: 457 us
  waiting for transfers between devices  211 us (46%)
  blocking collectives  130 us (28%)
  matrix products  36.4 us (8%)
  local copies, waits for them, and re-layouts  27.5 us (6%)
  starting transfers between devices  23.5 us (5%)
  between operations  15 us (3%)
  other arithmetic  14 us (3%)
    reduce_scatter x1, waiting for transfers between devices, on_device(): lax.psum_scatter(prompt_term(score_stack, weight_stack, query_heads, grad...  195 us
    all_gather x1, blocking collectives, on_device(): lax.all_gather(prompt_key, 'seq', axis=0, tiled=True)  68.1 us
    all_gather x1, blocking collectives, on_device(): lax.all_gather(prompt_value, 'seq', axis=0, tiled=True)  61.6 us
    ppermute x9, starting transfers between devices, passed_along(): return lax.ppermute(value, axis, pairs)  23.5 us
    ppermute x9, waiting for transfers between devices, passed_along(): return lax.ppermute(value, axis, pairs)  15.8 us
    unnamed x80, local copies, waits for them, and re-layouts  9.48 us
  transfers between devices with their start and end apart: 10, of which 4 were waited for; matrix products, arithmetic and copies ran while one was open for 6% of the time, Pallas kernels for 0%

commit v1 on v0

v1 whole, which is shorter than its diff:
```python
import math

import jax
import jax.numpy as jnp
from jax import lax
from jax.experimental import pallas as pl
from jax.experimental.pallas import tpu as pltpu
from jax.sharding import PartitionSpec as P

MESH = pl.DeviceIdType.MESH
HD = 128
HK = 4
GROUP = 8
PAIRS = GROUP // 2
SCALE = HD ** (-0.5)
EXP_SCALE = SCALE * math.log2(math.e)
BF = jnp.bfloat16
F32 = jnp.float32


def body(
    nz,
    q_ref,
    rk_ref,
    rv_ref,
    pk_ref,
    pv_ref,
    do_ref,
    seg_ref,
    dq_ref,
    drk_ref,
    drv_ref,
    dpk_ref,
    dpv_ref,
    qt,
    dot,
    win,
    gat,
    bias,
    pr,
    dpr,
    mr,
    lr,
    sp,
    dpp,
    kp,
    vp,
    kt,
    pt,
    dst,
    ps,
    pf,
    rc,
    xs,
    xf,
    rx,
    zs,
    zf,
    rz,
    tb,
    tf,
    rp,
    ts,
    ra,
    rb,
    s_kv,
    r_kv,
    s_one,
    r_one,
):
    n = 4 * nz
    keys = 4 * HD
    npr = 32 * nz
    total = keys + npr
    me = lax.axis_index("seq")
    grp = lax.axis_index("grp")
    core = me % 2
    x = (me // 2) % 2
    z = me // 4
    peer = me + 1 - 2 * core
    xpeer = me + 2 - 4 * x

    def zpeer(d):
        return ((z + d) % nz) * 4 + me % 4

    def device(index):
        return (grp, index)

    GZ, GX, GC, PC, PX, PZ, TP, TB, TA = range(9)

    def copy(src, dst, kind, g, to):
        return pltpu.make_async_remote_copy(
            src_ref=src,
            dst_ref=dst,
            send_sem=s_one.at[kind, g],
            recv_sem=r_one.at[kind, g],
            device_id=device(to),
            device_id_type=MESH,
        )

    barrier = pltpu.get_barrier_semaphore()

    def greet(to):
        pl.semaphore_signal(barrier, inc=1, device_id=device(to), device_id_type=MESH)

    greet(peer)
    greet(xpeer)
    greet((me + 2) % n)
    greet((me + n - 2) % n)
    greet((me + n + 6 * core - 3) % n)

    def greet_z(d, carry):
        greet(zpeer(d))
        return carry

    lax.fori_loop(1, nz, greet_z, 0)

    labels = jnp.broadcast_to((seg_ref[...] + 1).astype(F32), (16, HD)).astype(BF)
    for g in range(HK):
        cols = slice(g * HD, (g + 1) * HD)
        win[g, 0, 0:HD, :] = rk_ref[:, cols]
        win[g, 0, HD : 2 * HD, :] = rv_ref[:, cols]
        win[g, 0, 2 * HD : 2 * HD + 16, :] = labels
        gat[g, core, x, z] = jnp.concatenate(
            (pk_ref[:, cols].astype(F32), pv_ref[:, cols].astype(F32)), axis=0
        ).astype(BF)
    pl.semaphore_wait(barrier, 5 + nz - 1)

    def block(g, slot):
        return win.at[g, slot, pl.ds(0, 2 * HD + (16 if g == 0 else 0))]

    def kv_copy(g, which, from_slot, to_slot, to):
        return pltpu.make_async_remote_copy(
            src_ref=block(g, from_slot),
            dst_ref=block(g, to_slot),
            send_sem=s_kv.at[g, which],
            recv_sem=r_kv.at[g, to_slot],
            device_id=device(to),
            device_id_type=MESH,
        )

    def kv_far(g):
        return kv_copy(g, 0, 0, 2, (me + 2) % n)

    def kv_side(g):
        return kv_copy(g, 1, 0, 1 + 2 * core, (me + 1 + 2 * core) % n)

    def kv_pass(g):
        return kv_copy(g, 2, 2, 3 - 2 * core, peer)

    def kv_forward(g):
        kv_far(g).wait_recv()
        kv_pass(g).start()

    def kv_ready(g):
        kv_copy(g, 1, 0, 1, peer).wait_recv()
        kv_copy(g, 1, 0, 3, peer).wait_recv()

    def gz_start(g):
        def step(d, carry):
            copy(gat.at[g, core, x, z], gat.at[g, core, x, z], GZ, g, zpeer(d)).start()
            return carry

        lax.fori_loop(1, nz, step, 0)

    def gz_all(g):
        part = gat.at[g, core, x, pl.ds(0, nz - 1)]
        return copy(part, part, GZ, g, peer)

    def gx_copy(g):
        return copy(gat.at[g, core, x], gat.at[g, core, x], GX, g, xpeer)

    def gc_copy(g):
        return copy(gat.at[g, core], gat.at[g, core], GC, g, peer)

    def gather_x(g):
        gz_all(g).wait_recv()
        gx_copy(g).start()

    def gather_c(g):
        gx_copy(g).wait_recv()
        gc_copy(g).start()

    for g in range(HK):
        kv_far(g).start()
        kv_side(g).start()
        gz_start(g)

    def flip(h, carry):
        cols = pl.ds(pl.multiple_of(h * HD, HD), HD)
        qt[:, cols] = q_ref[:, cols].T
        dot[:, cols] = do_ref[:, cols].T
        return carry

    lax.fori_loop(0, HK * GROUP, flip, 0)

    def make_bias():
        mine = jnp.broadcast_to(win[0, 0, 2 * HD : 2 * HD + 16, :].astype(F32)[0:1], (HD, HD))
        row = lax.broadcasted_iota(jnp.int32, (HD, HD), 1)
        col = lax.broadcasted_iota(jnp.int32, (HD, HD), 0)
        for slot in range(4):
            theirs = jnp.broadcast_to(
                win[0, slot, 2 * HD : 2 * HD + 16, :].astype(F32)[0:1], (HD, HD)
            ).T
            seen = mine == theirs
            if slot == 0:
                seen = seen & (col <= row)
            else:
                seen = seen & (jnp.broadcast_to(me, (HD, HD)) >= slot)
            bias[slot] = jnp.where(seen, 0.0, -jnp.inf)

    def fold(value, op):
        return op(value.reshape(value.shape[0] // 8, 8, value.shape[1]), axis=0)

    def unit_cols(g, u):
        return pl.ds(pl.multiple_of((g * PAIRS + u) * 2 * HD, 2 * HD), 2 * HD)

    def resp_unit(g, u):
        unit = g * PAIRS + u
        cols = unit_cols(g, u)
        q2 = qt[:, cols]
        do2 = dot[:, cols]
        high = None
        for slot in range(4):
            mask = bias[slot]
            part = jnp.dot(win[g, slot, 0:HD, :], q2, preferred_element_type=F32)
            part = part + jnp.concatenate((mask, mask), axis=1)
            pr[unit, slot] = part
            top = fold(part, jnp.max)
            high = top if high is None else jnp.maximum(high, top)
            dpr[unit, slot] = jnp.dot(
                win[g, slot, HD : 2 * HD, :], do2, preferred_element_type=F32
            )
        high = jnp.max(high, axis=0, keepdims=True)
        low = None
        for slot in range(4):
            part = jnp.exp2((pr[unit, slot] - high) * EXP_SCALE)
            pr[unit, slot] = part
            add = fold(part, jnp.sum)
            low = add if low is None else low + add
        mr[unit] = jnp.broadcast_to(high, (8, 2 * HD))
        lr[unit] = jnp.broadcast_to(jnp.sum(low, axis=0, keepdims=True), (8, 2 * HD))

    def prompt_ready(g):
        gc_copy(g).wait_recv()
        all_rows = gat[g].reshape(4 * nz, 16, HD).astype(F32)
        kp[...] = all_rows[:, 0:8].reshape(npr, HD).astype(BF)
        vp[...] = all_rows[:, 8:16].reshape(npr, HD).astype(BF)
        for slot in range(4):
            kt[:, slot * HD : (slot + 1) * HD] = win[g, slot, 0:HD, :].T
        for lower in range(0, npr, HD):
            width = min(HD, npr - lower)
            kt[:, keys + lower : keys + lower + width] = kp[lower : lower + width, :].T

    chunk = min(HD, npr)
    chunks = npr // chunk

    def full_unit(g, u):
        unit = g * PAIRS + u
        cols = unit_cols(g, u)
        own = pl.ds(pl.multiple_of(u * 2 * HD, 2 * HD), 2 * HD)
        q2 = qt[:, cols]
        do2 = dot[:, cols]
        high = mr[unit]
        for c in range(chunks):
            rows = slice(c * chunk, (c + 1) * chunk)
            part = jnp.dot(kp[rows, :], q2, preferred_element_type=F32)
            sp[rows, :] = part
            high = jnp.maximum(high, fold(part, jnp.max))
            dpp[rows, :] = jnp.dot(vp[rows, :], do2, preferred_element_type=F32)
        old = mr[unit][0:1]
        high = jnp.max(high, axis=0, keepdims=True)
        low = None
        for c in range(chunks):
            rows = slice(c * chunk, (c + 1) * chunk)
            part = jnp.exp2((sp[rows, :] - high) * EXP_SCALE)
            sp[rows, :] = part
            add = fold(part, jnp.sum)
            low = add if low is None else low + add
        shrink = jnp.exp2((old - high) * EXP_SCALE)
        sums = jnp.sum(low, axis=0, keepdims=True) + lr[unit][0:1] * shrink
        f_prompt = 1.0 / sums
        f_resp = shrink * f_prompt
        delta = None
        for slot in range(4):
            rounded = (pr[unit, slot] * f_resp).astype(BF)
            pt[slot * HD : (slot + 1) * HD, own] = rounded
            add = fold(rounded.astype(F32) * dpr[unit, slot], jnp.sum)
            delta = add if delta is None else delta + add
        for c in range(chunks):
            rows = slice(c * chunk, (c + 1) * chunk)
            rounded = (sp[rows, :] * f_prompt).astype(BF)
            pt[keys + c * chunk : keys + (c + 1) * chunk, own] = rounded
            delta = delta + fold(rounded.astype(F32) * dpp[rows, :], jnp.sum)
        delta = jnp.sum(delta, axis=0, keepdims=True)
        for slot in range(4):
            dst[slot * HD : (slot + 1) * HD, own] = (
                (pr[unit, slot] * f_resp) * (dpr[unit, slot] - delta)
            ).astype(BF)
        for c in range(chunks):
            rows = slice(c * chunk, (c + 1) * chunk)
            dst[keys + c * chunk : keys + (c + 1) * chunk, own] = (
                (sp[rows, :] * f_prompt) * (dpp[rows, :] - delta)
            ).astype(BF)

    def head_grads(g):
        heads = range(g * GROUP, (g + 1) * GROUP)
        q_rows = jnp.concatenate([q_ref[:, h * HD : (h + 1) * HD] for h in heads], axis=0)
        do_rows = jnp.concatenate([do_ref[:, h * HD : (h + 1) * HD] for h in heads], axis=0)
        for lower in range(0, npr, chunk):
            rows = slice(keys + lower, keys + lower + chunk)
            dk = jnp.dot(dst[rows, :], q_rows, preferred_element_type=F32) * SCALE
            dv = jnp.dot(pt[rows, :], do_rows, preferred_element_type=F32)
            blocks = chunk // 8
            both = jnp.concatenate(
                (dk.reshape(blocks, 8, HD), dv.reshape(blocks, 8, HD)), axis=1
            )
            first = lower // 8
            pf[g, first : first + blocks] = both
            ps[g, first : first + blocks] = both.astype(BF)
        pc_copy(g).start()
        for slot in range(4):
            rows = slice(slot * HD, (slot + 1) * HD)
            dk = jnp.dot(dst[rows, :], q_rows, preferred_element_type=F32) * SCALE
            dv = jnp.dot(pt[rows, :], do_rows, preferred_element_type=F32)
            if slot in (0, 2):
                tf[g, slot // 2, 0:HD, :] = dk
                tf[g, slot // 2, HD : 2 * HD, :] = dv
            else:
                tb[g, slot // 2, 0:HD, :] = dk.astype(BF)
                tb[g, slot // 2, HD : 2 * HD, :] = dv.astype(BF)
        tp_copy(g).start()
        tb_copy(g).start()

    def head_query(g):
        for j in range(PAIRS):
            part = jnp.dot(
                kt[...], dst[:, j * 2 * HD : (j + 1) * 2 * HD], preferred_element_type=F32
            )
            for i in range(2):
                h = g * GROUP + j * 2 + i
                dq_ref[:, h * HD : (h + 1) * HD] = (
                    part[:, i * HD : (i + 1) * HD].T * SCALE
                ).astype(BF)

    half = 2 * nz

    def pc_copy(g):
        return copy(ps.at[g, pl.ds((1 - core) * half, half)], rc.at[g], PC, g, peer)

    def px_copy(g):
        return copy(xs.at[g], rx.at[g], PX, g, xpeer)

    def px_send(g):
        pc_copy(g).wait_recv()
        away = 1 - x
        xs[g] = (
            pf[g, pl.ds(core * half + away * nz, nz)]
            + rc[g, pl.ds(away * nz, nz)].astype(F32)
        ).astype(BF)
        xf[g] = pf[g, pl.ds(core * half + x * nz, nz)] + rc[g, pl.ds(x * nz, nz)].astype(F32)
        px_copy(g).start()

    def pz_send(g):
        px_copy(g).wait_recv()
        sums = xf[g] + rx[g].astype(F32)
        zf[g] = sums
        zs[g] = sums.astype(BF)

        def step(d, carry):
            copy(zs.at[g, (z + d) % nz], rz.at[g, d - 1], PZ, g, zpeer(d)).start()
            return carry

        lax.fori_loop(1, nz, step, 0)

    def pz_all(g):
        return copy(zs.at[g, pl.ds(0, nz - 1)], rz.at[g], PZ, g, peer)

    def prompt_out(g):
        pz_all(g).wait_recv()
        sums = zf[g, z] + jnp.sum(rz[g].astype(F32), axis=0)
        cols = slice(g * HD, (g + 1) * HD)
        dpk_ref[:, cols] = sums[0:8]
        dpv_ref[:, cols] = sums[8:16]

    def tp_copy(g):
        return copy(tb.at[g, core], rp.at[g], TP, g, peer)

    def tb_copy(g):
        return copy(tb.at[g, 1 - core], rb.at[g], TB, g, (me + n - 3 + 2 * core) % n)

    def ta_copy(g):
        return copy(ts.at[g], ra.at[g], TA, g, (me + n - 2) % n)

    def ts_send(g):
        tp_copy(g).wait_recv()
        ts[g] = (tf[g, 1] + rp[g].astype(F32)).astype(BF)
        ta_copy(g).start()

    def resp_out(g):
        ta_copy(g).wait_recv()
        tb_copy(g).wait_recv()
        sums = tf[g, 0] + ra[g].astype(F32) + rb[g].astype(F32)
        cols = slice(g * HD, (g + 1) * HD)
        drk_ref[:, cols] = sums[0:HD]
        drv_ref[:, cols] = sums[HD : 2 * HD]

    def run(unit, g, lower, upper):
        def step(u, carry):
            unit(g, u)
            return carry

        lax.fori_loop(lower, upper, step, 0)

    kv_forward(0)
    for g in range(HK):
        if g + 1 < HK:
            kv_forward(g + 1)
        kv_ready(g)
        if g == 0:
            make_bias()
        run(resp_unit, g, 0, PAIRS)
        if g >= 2:
            gather_c(g - 2)
        if g >= 1:
            gather_x(g - 1)
    for g in range(HK):
        if g == 1:
            gather_c(HK - 1)
        prompt_ready(g)
        run(full_unit, g, 0, 2)
        if g == 0:
            gather_c(HK - 2)
            gather_x(HK - 1)
        else:
            px_send(g - 1)
            ts_send(g - 1)
        run(full_unit, g, 2, PAIRS)
        if g > 0:
            pz_send(g - 1)
        head_grads(g)
        head_query(g)
    last = HK - 1
    px_send(last)
    ts_send(last)
    for g in range(last):
        prompt_out(g)
        resp_out(g)
    pz_send(last)
    resp_out(last)
    prompt_out(last)

    for g in range(HK):
        kv_far(g).wait_send()
        kv_side(g).wait_send()
        kv_pass(g).wait_send()
        gz_all(g).wait_send()
        gx_copy(g).wait_send()
        gc_copy(g).wait_send()
        pc_copy(g).wait_send()
        px_copy(g).wait_send()
        pz_all(g).wait_send()
        tp_copy(g).wait_send()
        tb_copy(g).wait_send()
        ta_copy(g).wait_send()


def on_device(queries, resp_key, resp_value, prompt_key, prompt_value, out_grad, segment):
    n = lax.axis_size("seq")
    nz = n // 4
    rows = queries.shape[0]
    npr = 32 * nz
    total = 4 * HD + npr
    units = HK * PAIRS
    vmem = pl.BlockSpec(memory_space=pltpu.VMEM)
    scratch = [
        ((HD, HK * GROUP * HD), BF),
        ((HD, HK * GROUP * HD), BF),
        ((HK, 4, 2 * HD + 16, HD), BF),
        ((HK, 2, 2, nz, 16, HD), BF),
        ((4, HD, HD), F32),
        ((units, 4, HD, 2 * HD), F32),
        ((units, 4, HD, 2 * HD), F32),
        ((units, 8, 2 * HD), F32),
        ((units, 8, 2 * HD), F32),
        ((npr, 2 * HD), F32),
        ((npr, 2 * HD), F32),
        ((npr, HD), BF),
        ((npr, HD), BF),
        ((HD, total), BF),
        ((total, GROUP * HD), BF),
        ((total, GROUP * HD), BF),
        ((HK, 4 * nz, 16, HD), BF),
        ((HK, 4 * nz, 16, HD), F32),
        ((HK, 2 * nz, 16, HD), BF),
        ((HK, nz, 16, HD), BF),
        ((HK, nz, 16, HD), F32),
        ((HK, nz, 16, HD), BF),
        ((HK, nz, 16, HD), BF),
        ((HK, nz, 16, HD), F32),
        ((HK, nz - 1, 16, HD), BF),
        ((HK, 2, 2 * HD, HD), BF),
        ((HK, 2, 2 * HD, HD), F32),
        ((HK, 2 * HD, HD), BF),
        ((HK, 2 * HD, HD), BF),
        ((HK, 2 * HD, HD), BF),
        ((HK, 2 * HD, HD), BF),
    ]
    return tuple(
        pl.pallas_call(
            lambda *refs: body(nz, *refs),
            out_shape=[
                jax.ShapeDtypeStruct((rows, HK * GROUP * HD), BF),
                jax.ShapeDtypeStruct((rows, HK * HD), F32),
                jax.ShapeDtypeStruct((rows, HK * HD), F32),
                jax.ShapeDtypeStruct((8, HK * HD), F32),
                jax.ShapeDtypeStruct((8, HK * HD), F32),
            ],
            in_specs=[vmem] * 7,
            out_specs=[vmem] * 5,
            scratch_shapes=[pltpu.VMEM(shape, kind) for shape, kind in scratch]
            + [
                pltpu.SemaphoreType.DMA((HK, 3)),
                pltpu.SemaphoreType.DMA((HK, 4)),
                pltpu.SemaphoreType.DMA((9, HK)),
                pltpu.SemaphoreType.DMA((9, HK)),
            ],
            compiler_params=pltpu.CompilerParams(
                collective_id=0, has_side_effects=True, vmem_limit_bytes=56 * 1024 * 1024
            ),
            cost_estimate=pl.CostEstimate(
                flops=6 * 10**9, bytes_accessed=6 * 10**6, transcendentals=4 * 10**6
            ),
            name="attention_backward",
        )(
            queries,
            resp_key,
            resp_value,
            prompt_key,
            prompt_value,
            out_grad,
            segment.reshape(1, rows),
        )
    )


def solution(mesh):
    spec = P(("grp", "seq"), None)
    return jax.shard_map(
        on_device,
        mesh=mesh,
        in_specs=(spec,) * 6 + (P(("grp", "seq")),),
        out_specs=(spec,) * 5,
        check_vma=False,
    )
```

time: 458 us -> 91.4 us (0.20)
  waiting for transfers between devices: 211 us -> 0 us
  blocking collectives: 130 us -> 0 us
  Pallas kernels: 0 us -> 83.6 us
  matrix products: 36.4 us -> 0 us
  starting transfers between devices: 23.5 us -> 0 us
  local copies, waits for them, and re-layouts: 27.5 us -> 5.42 us
  between operations: 15 us -> 0.66 us
  other arithmetic: 14 us -> 0 us
    reduce_scatter x1 -> x0, waiting for transfers between devices: 195 us -> none  [on_device(): lax.psum_scatter(prompt_term(score_stack, weight_stack, query_heads, grad...]
    all_gather x2 -> x0, blocking collectives: 130 us -> none  [the longest x1 68.1 us: on_device(): lax.all_gather(prompt_key, 'seq', axis=0, tiled=True)]
    pallas_call x0 -> x1, Pallas kernels: none -> 83.6 us  [on_device(): pl.pallas_call(lambda *refs: body(nz, *refs), out_shape=[jax.ShapeDtypeSt...]
    dot_general x26 -> x0, matrix products: 36.4 us -> none  [the longest x4 8.57 us: head_terms(): jnp.einsum('rgd,nd->grn', head_grads, head_values, preferred_element_type...]
    ppermute x9 -> x0, starting transfers between devices: 23.5 us -> none  [passed_along(): return lax.ppermute(value, axis, pairs)]
    ppermute x9 -> x0, waiting for transfers between devices: 15.8 us -> none  [passed_along(): return lax.ppermute(value, axis, pairs)]
    reshape x6 -> x0, local copies, waits for them, and re-layouts: 9.68 us -> none  [the longest x4 4.58 us: attend_block(): grad_query.append(results[0].reshape(row_count, group_size * HD))]
    another operation x10 -> x0, local copies, waits for them, and re-layouts: 5.35 us -> none  [the longest x4 4.94 us: attend_block(): jnp.stack(score_parts)]
  transfers between devices with their start and end apart: 10 -> 0, of which waited for: 4 -> 0; matrix products, arithmetic and copies ran while one was open for 6% -> 0% of each run, Pallas kernels for 0% -> 0%
where the time goes in v1:
time: 91.4 us; the launch traced here: 89.7 us
  Pallas kernels  83.6 us (91%)
  local copies, waits for them, and re-layouts  5.42 us (6%)
    pallas_call x1, Pallas kernels, on_device(): pl.pallas_call(lambda *refs: body(nz, *refs), out_shape=[jax.ShapeDtypeSt...  83.6 us
    unnamed x13, local copies, waits for them, and re-layouts  5.42 us

profile of v1, /device:TPU:24, one launch (start us, length us, event | category | flops | bytes accessed | tf_op | source)
XLA Modules:
  0.0 89.7 jit_solution(16546636490246374579)
XLA Ops:
  0.6 83.6 %attention_backward.1 = (bf16[128,4096]{1,0:T(8,128)(2,1)}, f32[128,512]{1,0:T(8,128)}, f32[128,512]{1,0:T(8,128)}, f32[8,512]{1,0:T(8,128)}, f32[8,512]{1,0:T(8,128)}) custom-call(bf16[128,4096]{1,0:T(8,128)(2,1)} %refs_0_.1, bf16[128,512]{1,0:T(8,128)(2,1)} %refs_1_.1, bf16[128,512]{1,0:T(8,128)(2,1)} %refs_2_.1, bf16[8,512]{1,0:T(8,128)(2,1)} %refs_3_.1, ...), custom_call_target="tpu_custom_call" | custom-call | flops 6000000000 | bytes 6000000 | tf_op jit(solution)/shard_map/attention_backward/pallas_call | solution.py:510
  84.3 0.0 copy-start.1
  84.3 2.3 %copy.17 = bf16[128,4096]{1,0:T(8,128)(2,1)} copy(bf16[128,4096]{1,0:T(8,128)(2,1)} %get-tuple-element.10) | data formatting | bytes 2097152
  86.6 0.0 copy-done.1
  86.6 0.0 copy-start
  86.6 0.7 copy.18
  87.3 0.3 copy-done
  87.6 0.0 copy-start.3
  87.6 0.7 copy.19
  88.4 0.0 copy-done.3
  88.4 0.0 copy-start.2
  88.4 0.6 copy.20
  89.0 0.1 copy-done.2
  89.1 0.6 copy.21
Async XLA Ops:
  84.3 2.3 %copy-start.1 = (f32[128,512]{1,0:T(8,128)S(1)}, f32[128,512]{1,0:T(8,128)}, u32[]{:S(2)}) copy-start(f32[128,512]{1,0:T(8,128)} %get-tuple-element.11) | copy-start | bytes 786436
  86.6 1.0 %copy-start = (f32[128,512]{1,0:T(8,128)S(1)}, f32[128,512]{1,0:T(8,128)}, u32[]{:S(2)}) copy-start(f32[128,512]{1,0:T(8,128)} %get-tuple-element.12) | copy-start | bytes 786436
  87.6 0.7 copy-start.3
  88.4 0.7 copy-start.2

commit v2 on v1

v2 whole, which is shorter than its diff:
```python
import math

import jax
import jax.numpy as jnp
from jax import lax
from jax.experimental import pallas as pl
from jax.experimental.pallas import tpu as pltpu
from jax.sharding import PartitionSpec as P

MESH = pl.DeviceIdType.MESH
HD = 128
HK = 4
GROUP = 8
PAIRS = GROUP // 2
SCALE = HD ** (-0.5)
EXP_SCALE = SCALE * math.log2(math.e)
BF = jnp.bfloat16
F32 = jnp.float32


def body(
    nz,
    q_hbm,
    rk_ref,
    rv_ref,
    pk_ref,
    pv_ref,
    do_hbm,
    seg_ref,
    dq_hbm,
    drk_ref,
    drv_ref,
    dpk_ref,
    dpv_ref,
    q_ref,
    do_ref,
    dq_ref,
    qt,
    dot,
    win,
    gat,
    bias,
    pr_a,
    pr_b,
    dpr_a,
    dpr_b,
    mr,
    lr,
    sp_a,
    sp_b,
    dpp_a,
    dpp_b,
    kp,
    vp,
    kt,
    pt,
    dst,
    dk_acc,
    dv_acc,
    ps,
    pf,
    rc,
    xs,
    xf,
    rx,
    zs,
    zf,
    rz,
    tb,
    tf,
    rp,
    ts,
    ra,
    rb,
    s_kv,
    r_kv,
    s_ring,
    r_ring,
    s_one,
    r_one,
    s_in,
    s_out,
):
    n = 4 * nz
    keys = 4 * HD
    npr = 32 * nz
    total = keys + npr
    quads = 2 * HK
    wide = 4 * HD
    me = lax.axis_index("seq")
    grp = lax.axis_index("grp")
    core = lax.rem(me, 2)
    x = lax.rem(lax.div(me, 2), 2)
    z = lax.div(me, 4)
    peer = me + 1 - 2 * core
    xpeer = me + 2 - 4 * x

    def zpeer(d):
        return lax.rem(me + 4 * d, n)

    def device(index):
        return (grp, index)

    GX, GC, PC, PX, PZ, TP, TB, TA = range(8)

    def copy(src, dst, kind, g, to):
        return pltpu.make_async_remote_copy(
            src_ref=src,
            dst_ref=dst,
            send_sem=s_one.at[kind, g],
            recv_sem=r_one.at[kind, g],
            device_id=device(to),
            device_id_type=MESH,
        )

    barrier = pltpu.get_barrier_semaphore()

    def greet(to):
        pl.semaphore_signal(barrier, inc=1, device_id=device(to), device_id_type=MESH)

    greet(peer)
    greet(xpeer)
    greet(lax.rem(me + 2, n))
    greet(lax.rem(me + n - 2, n))
    greet(lax.rem(me + n + 6 * core - 3, n))

    def greet_z(d, carry):
        greet(zpeer(d))
        return carry

    lax.fori_loop(1, nz, greet_z, 0)
    q_in = pltpu.make_async_copy(q_hbm, q_ref, s_in.at[0])
    do_in = pltpu.make_async_copy(do_hbm, do_ref, s_in.at[1])
    q_in.start()
    do_in.start()

    labels = jnp.broadcast_to((seg_ref[...] + 1).astype(F32), (16, HD)).astype(BF)
    for g in range(HK):
        cols = slice(g * HD, (g + 1) * HD)
        win[g, 0, 0:HD, :] = rk_ref[:, cols]
        win[g, 0, HD : 2 * HD, :] = rv_ref[:, cols]
        win[g, 0, 2 * HD : 2 * HD + 16, :] = labels
        gat[core, x, z, g] = jnp.concatenate(
            (pk_ref[:, cols].astype(F32), pv_ref[:, cols].astype(F32)), axis=0
        ).astype(BF)
    pl.semaphore_wait(barrier, 5 + nz - 1)

    def kv_copy(g, which, from_slot, to_slot, to):
        return pltpu.make_async_remote_copy(
            src_ref=win.at[g, from_slot],
            dst_ref=win.at[g, to_slot],
            send_sem=s_kv.at[g, which],
            recv_sem=r_kv.at[g, to_slot],
            device_id=device(to),
            device_id_type=MESH,
        )

    def kv_far(g):
        return kv_copy(g, 0, 0, 2, lax.rem(me + 2, n))

    def kv_side(g):
        return kv_copy(g, 1, 0, 1 + 2 * core, lax.rem(me + 1 + 2 * core, n))

    def kv_pass(g):
        return kv_copy(g, 2, 2, 3 - 2 * core, peer)

    def kv_forward(g):
        kv_far(g).wait_recv()
        kv_pass(g).start()

    def kv_ready(g):
        kv_copy(g, 1, 0, 1, peer).wait_recv()
        kv_copy(g, 1, 0, 3, peer).wait_recv()

    steps = nz // 4

    def ring_copy(owner, to, d):
        part = gat.at[core, x, owner]
        return pltpu.make_async_remote_copy(
            src_ref=part,
            dst_ref=part,
            send_sem=s_ring.at[0],
            recv_sem=r_ring.at[d],
            device_id=device(to),
            device_id_type=MESH,
        )

    def ring_wait(d):
        ring_copy(lax.rem(z + nz - d, nz), peer, d).wait_recv()

    def ring_step(k):
        if k > 1:
            ring_wait(2 * (k - 1))
            ring_wait(nz - 2 * (k - 1))
        up = lax.rem(z + nz - 2 * (k - 1), nz)
        down = lax.rem(z + 2 * (k - 1), nz)
        ring_copy(up, zpeer(2), 2 * k).start()
        if k < steps:
            ring_copy(down, zpeer(nz - 2), nz - 2 * k).start()
        ring_copy(up, zpeer(1), 2 * k - 1).start()
        ring_copy(down, zpeer(nz - 1), nz - 2 * k + 1).start()

    def gx_copy(g):
        part = gat.at[core, x, pl.ds(0, nz), g]
        return copy(part, part, GX, g, xpeer)

    def gc_copy(g):
        part = gat.at[core, pl.ds(0, 2), pl.ds(0, nz), g]
        return copy(part, part, GC, g, peer)

    def ring_end():
        for k in range(1, steps + 1):
            ring_wait(2 * k - 1)
            ring_wait(nz - 2 * k + 1)
        ring_wait(2 * steps)

    def gather_x(g):
        gx_copy(g).start()

    def gather_c(g):
        gx_copy(g).wait_recv()
        gc_copy(g).start()

    def kv_send(g):
        kv_far(g).start()
        kv_side(g).start()

    kv_send(0)
    ring_step(1)
    kv_send(1)

    q_in.wait()
    do_in.wait()

    def flip(h, carry):
        for i in range(4):
            cols = pl.ds(pl.multiple_of((h * 4 + i) * HD, HD), HD)
            qt[:, cols] = q_ref[:, cols].T
            dot[:, cols] = do_ref[:, cols].T
        return carry

    lax.fori_loop(0, HK * GROUP // 8, flip, 0)
    ring_step(2)
    lax.fori_loop(HK * GROUP // 8, HK * GROUP // 4, flip, 0)
    kv_forward(0)
    ring_step(3)

    def make_bias():
        mine = jnp.broadcast_to(win[0, 0, 2 * HD : 2 * HD + 16, :].astype(F32)[0:1], (HD, HD))
        row = lax.broadcasted_iota(jnp.int32, (HD, HD), 1)
        col = lax.broadcasted_iota(jnp.int32, (HD, HD), 0)
        for slot in range(4):
            theirs = jnp.broadcast_to(
                win[0, slot, 2 * HD : 2 * HD + 16, :].astype(F32)[0:1], (HD, HD)
            ).T
            seen = mine == theirs
            if slot == 0:
                seen = seen & (col <= row)
            else:
                seen = seen & (jnp.broadcast_to(me, (HD, HD)) >= slot)
            bias[slot] = jnp.where(seen, 0.0, -jnp.inf)

    def fold(value, op):
        return op(value.reshape(value.shape[0] // 8, 8, value.shape[1]), axis=0)

    def half_cols(quad, half):
        return pl.ds(pl.multiple_of(quad * wide + half * 2 * HD, 2 * HD), 2 * HD)

    def quad_cols(quad):
        return pl.ds(pl.multiple_of(quad * wide, wide), wide)

    def resp_half(quad, half, pr, dpr):
        g = lax.div(quad, 2)
        cols = half_cols(quad, half)
        k4 = win[g, :, 0:HD, :].reshape(keys, HD)
        v4 = win[g, :, HD : 2 * HD, :].reshape(keys, HD)
        scores = jnp.dot(k4, qt[:, cols], preferred_element_type=F32)
        high = None
        for slot in range(4):
            mask = bias[slot]
            part = scores[slot * HD : (slot + 1) * HD] + jnp.concatenate((mask, mask), axis=1)
            pr[quad, slot] = part
            top = fold(part, jnp.max)
            high = top if high is None else jnp.maximum(high, top)
        high = jnp.max(high, axis=0, keepdims=True)
        dpr[quad] = jnp.dot(v4, dot[:, cols], preferred_element_type=F32).reshape(4, HD, 2 * HD)
        low = None
        for slot in range(4):
            part = jnp.exp2((pr[quad, slot] - high) * EXP_SCALE)
            pr[quad, slot] = part
            add = fold(part, jnp.sum)
            low = add if low is None else low + add
        mr[quad, half] = jnp.broadcast_to(high, (8, 2 * HD))
        lr[quad, half] = jnp.broadcast_to(jnp.sum(low, axis=0, keepdims=True), (8, 2 * HD))

    def prompt_ready(g):
        gc_copy(g).wait_recv()
        all_rows = gat[:, :, :, g].reshape(4 * nz, 16, HD).astype(F32)
        kp[g] = all_rows[:, 0:8].reshape(npr, HD).astype(BF)
        vp[g] = all_rows[:, 8:16].reshape(npr, HD).astype(BF)
        for slot in range(4):
            kt[g, :, slot * HD : (slot + 1) * HD] = win[g, slot, 0:HD, :].T
        for lower in range(0, npr, HD):
            kt[g, :, keys + lower : keys + lower + HD] = kp[g, lower : lower + HD, :].T

    chunks = npr // HD

    def full_half(quad, half, pr, dpr, sp, dpp):
        g = lax.div(quad, 2)
        cols = half_cols(quad, half)
        own = slice(half * 2 * HD, (half + 1) * 2 * HD)
        scores = jnp.dot(kp[g], qt[:, cols], preferred_element_type=F32)
        sp[...] = scores
        high = jnp.maximum(mr[quad, half], fold(scores, jnp.max))
        dpp[...] = jnp.dot(vp[g], dot[:, cols], preferred_element_type=F32)
        old = mr[quad, half][0:1]
        high = jnp.max(high, axis=0, keepdims=True)
        low = None
        for c in range(chunks):
            rows = slice(c * HD, (c + 1) * HD)
            part = jnp.exp2((sp[rows, :] - high) * EXP_SCALE)
            sp[rows, :] = part
            add = fold(part, jnp.sum)
            low = add if low is None else low + add
        shrink = jnp.exp2((old - high) * EXP_SCALE)
        sums = jnp.sum(low, axis=0, keepdims=True) + lr[quad, half][0:1] * shrink
        f_prompt = 1.0 / sums
        f_resp = shrink * f_prompt
        delta = None
        for slot in range(4):
            rounded = (pr[quad, slot] * f_resp).astype(BF)
            pt[slot * HD : (slot + 1) * HD, own] = rounded
            add = fold(rounded.astype(F32) * dpr[quad, slot], jnp.sum)
            delta = add if delta is None else delta + add
        for c in range(chunks):
            rows = slice(c * HD, (c + 1) * HD)
            rounded = (sp[rows, :] * f_prompt).astype(BF)
            pt[keys + c * HD : keys + (c + 1) * HD, own] = rounded
            delta = delta + fold(rounded.astype(F32) * dpp[rows, :], jnp.sum)
        delta = jnp.sum(delta, axis=0, keepdims=True)
        for slot in range(4):
            dst[slot * HD : (slot + 1) * HD, own] = (
                (pr[quad, slot] * f_resp) * (dpr[quad, slot] - delta)
            ).astype(BF)
        for c in range(chunks):
            rows = slice(c * HD, (c + 1) * HD)
            dst[keys + c * HD : keys + (c + 1) * HD, own] = (
                (sp[rows, :] * f_prompt) * (dpp[rows, :] - delta)
            ).astype(BF)

    def full_quad(quad):
        full_half(quad, 0, pr_a, dpr_a, sp_a, dpp_a)
        full_half(quad, 1, pr_b, dpr_b, sp_b, dpp_b)

    def rows_of(ref, quad):
        part = ref[:, quad_cols(quad)]
        return jnp.concatenate([part[:, i * HD : (i + 1) * HD] for i in range(4)], axis=0)

    def add_keys(quad, lower, upper):
        second = lax.rem(quad, 2) == 1
        rows = slice(lower, upper)
        for acc, left, right in ((dv_acc, pt, do_ref), (dk_acc, dst, q_ref)):
            part = jnp.dot(left[rows, :], rows_of(right, quad), preferred_element_type=F32)
            acc[rows, :] = jnp.where(second, acc[rows, :], 0.0) + part

    def query_part(quad):
        g = lax.div(quad, 2)
        part = jnp.dot(kt[g], dst[...], preferred_element_type=F32)
        dq_ref[:, quad_cols(quad)] = jnp.concatenate(
            [(part[:, i * HD : (i + 1) * HD].T * SCALE).astype(BF) for i in range(4)], axis=1
        )

    def query_out(quad):
        cols = quad_cols(quad)
        return pltpu.make_async_copy(dq_ref.at[:, cols], dq_hbm.at[:, cols], s_out.at[quad])

    def emit_prompt(g):
        dk = dk_acc[keys:total, :] * SCALE
        dv = dv_acc[keys:total, :]
        both = jnp.concatenate(
            (dk.reshape(4 * nz, 8, HD), dv.reshape(4 * nz, 8, HD)), axis=1
        )
        pf[g] = both
        ps[g] = both.astype(BF)
        pc_copy(g).start()

    def emit_resp(g):
        for slot in range(4):
            rows = slice(slot * HD, (slot + 1) * HD)
            dk = dk_acc[rows, :] * SCALE
            dv = dv_acc[rows, :]
            if slot in (0, 2):
                tf[g, slot // 2, 0:HD, :] = dk
                tf[g, slot // 2, HD : 2 * HD, :] = dv
            else:
                tb[g, slot // 2, 0:HD, :] = dk.astype(BF)
                tb[g, slot // 2, HD : 2 * HD, :] = dv.astype(BF)
        tp_copy(g).start()
        tb_copy(g).start()

    half_blocks = 2 * nz

    def pc_copy(g):
        return copy(
            ps.at[g, pl.ds((1 - core) * half_blocks, half_blocks)], rc.at[g], PC, g, peer
        )

    def px_copy(g):
        return copy(xs.at[g], rx.at[g], PX, g, xpeer)

    def px_send(g):
        pc_copy(g).wait_recv()
        away = 1 - x
        xs[g] = (
            pf[g, pl.ds(core * half_blocks + away * nz, nz)]
            + rc[g, pl.ds(away * nz, nz)].astype(F32)
        ).astype(BF)
        xf[g] = (
            pf[g, pl.ds(core * half_blocks + x * nz, nz)] + rc[g, pl.ds(x * nz, nz)].astype(F32)
        )
        px_copy(g).start()

    def pz_send(g):
        px_copy(g).wait_recv()
        sums = xf[g] + rx[g].astype(F32)
        zf[g] = sums
        zs[g] = sums.astype(BF)

        for d in range(1, nz):
            copy(zs.at[g, lax.rem(z + d, nz)], rz.at[g, d - 1], PZ, g, zpeer(d)).start()

    def pz_all(g):
        return copy(zs.at[g, pl.ds(0, nz - 1)], rz.at[g], PZ, g, peer)

    def prompt_out(g):
        pz_all(g).wait_recv()
        sums = zf[g, z] + jnp.sum(rz[g].astype(F32), axis=0)
        cols = slice(g * HD, (g + 1) * HD)
        dpk_ref[:, cols] = sums[0:8]
        dpv_ref[:, cols] = sums[8:16]

    def tp_copy(g):
        return copy(tb.at[g, core], rp.at[g], TP, g, peer)

    def tb_copy(g):
        return copy(tb.at[g, 1 - core], rb.at[g], TB, g, lax.rem(me + n - 3 + 2 * core, n))

    def ta_copy(g):
        return copy(ts.at[g], ra.at[g], TA, g, lax.rem(me + n - 2, n))

    def ts_send(g):
        tp_copy(g).wait_recv()
        ts[g] = (tf[g, 1] + rp[g].astype(F32)).astype(BF)
        ta_copy(g).start()

    def resp_out(g):
        ta_copy(g).wait_recv()
        tb_copy(g).wait_recv()
        sums = tf[g, 0] + ra[g].astype(F32) + rb[g].astype(F32)
        cols = slice(g * HD, (g + 1) * HD)
        drk_ref[:, cols] = sums[0:HD]
        drv_ref[:, cols] = sums[HD : 2 * HD]

    def when(flag, *calls):
        @pl.when(flag)
        def _():
            for call, g in calls:
                call(g)

    def resp_quad(quad):
        resp_half(quad, 0, pr_a, dpr_a)
        resp_half(quad, 1, pr_b, dpr_b)

    kv_ready(0)
    make_bias()

    def resp_step(quad, carry):
        when(quad == 2, (kv_ready, 1))
        resp_quad(quad)
        when(quad == 0, (ring_step, 4), (kv_forward, 1))

        @pl.when(quad == 1)
        def _():
            ring_end()
            gather_x(0)
            kv_send(2)

        when(quad == 2, (gather_x, 1))
        when(quad == 3, (gather_c, 0), (kv_forward, 2), (kv_send, 3))
        return carry

    lax.fori_loop(0, 4, resp_step, 0)
    kv_ready(2)
    prompt_ready(0)
    resp_quad(4)
    full_quad(0)
    gather_c(1)
    gather_x(2)

    def both_step(quad, carry):
        when(quad == 6, (kv_ready, 3), (prompt_ready, 1))
        add_keys(quad - 5, 0, total)
        query_part(quad - 5)
        resp_quad(quad)
        full_quad(quad - 4)
        query_out(quad - 5).start()
        when(quad == 5, (kv_forward, 3), (gather_x, 3))
        when(quad == 6, (emit_prompt, 0), (emit_resp, 0), (gather_c, 2))
        when(quad == 7, (gather_c, 3), (px_send, 0), (ts_send, 0))
        return carry

    lax.fori_loop(5, quads, both_step, 0)

    def full_step(quad, carry):
        g = lax.div(quad, 2)
        first = lax.rem(quad, 2) == 0
        when(first, (prompt_ready, g))
        add_keys(quad - 1, 0, total)
        query_part(quad - 1)
        full_quad(quad)
        query_out(quad - 1).start()
        when(first, (emit_prompt, g - 1), (emit_resp, g - 1), (pz_send, g - 2))
        when(~first, (px_send, g - 1), (ts_send, g - 1))
        return carry

    lax.fori_loop(4, quads, full_step, 0)
    last = HK - 1
    add_keys(quads - 1, keys, total)
    emit_prompt(last)
    pz_send(last - 1)
    add_keys(quads - 1, 0, keys)
    emit_resp(last)
    query_part(quads - 1)
    query_out(quads - 1).start()
    px_send(last)
    ts_send(last)
    for g in range(last):
        prompt_out(g)
        resp_out(g)
    pz_send(last)
    resp_out(last)
    prompt_out(last)

    sent = gat.at[0, 0, pl.ds(0, nz - 1)]
    pltpu.make_async_remote_copy(
        src_ref=sent,
        dst_ref=sent,
        send_sem=s_ring.at[0],
        recv_sem=r_ring.at[0],
        device_id=device(peer),
        device_id_type=MESH,
    ).wait_send()
    for g in range(HK):
        kv_far(g).wait_send()
        kv_side(g).wait_send()
        kv_pass(g).wait_send()
        gx_copy(g).wait_send()
        gc_copy(g).wait_send()
        pc_copy(g).wait_send()
        px_copy(g).wait_send()
        pz_all(g).wait_send()
        tp_copy(g).wait_send()
        tb_copy(g).wait_send()
        ta_copy(g).wait_send()
    for quad in range(quads):
        query_out(quad).wait()


def hand_over(*refs):
    sems = refs[10]
    copies = [
        pltpu.make_async_copy(refs[i], refs[5 + i], sems.at[i]) for i in range(5)
    ]
    for one in copies:
        one.start()
    for one in copies:
        one.wait()


def on_device(queries, resp_key, resp_value, prompt_key, prompt_value, out_grad, segment):
    n = lax.axis_size("seq")
    nz = n // 4
    rows = queries.shape[0]
    npr = 32 * nz
    total = 4 * HD + npr
    quads = 2 * HK
    vmem = pl.BlockSpec(memory_space=pltpu.VMEM)
    whole = pl.BlockSpec(memory_space=pl.ANY)
    flat = HK * GROUP * HD
    scratch = [
        ((rows, flat), BF),
        ((rows, flat), BF),
        ((rows, flat), BF),
        ((HD, flat), BF),
        ((HD, flat), BF),
        ((HK, 4, 2 * HD + 16, HD), BF),
        ((2, 2, nz, HK, 16, HD), BF),
        ((4, HD, HD), F32),
        ((quads, 4, HD, 2 * HD), F32),
        ((quads, 4, HD, 2 * HD), F32),
        ((quads, 4, HD, 2 * HD), F32),
        ((quads, 4, HD, 2 * HD), F32),
        ((quads, 2, 8, 2 * HD), F32),
        ((quads, 2, 8, 2 * HD), F32),
        ((npr, 2 * HD), F32),
        ((npr, 2 * HD), F32),
        ((npr, 2 * HD), F32),
        ((npr, 2 * HD), F32),
        ((HK, npr, HD), BF),
        ((HK, npr, HD), BF),
        ((HK, HD, total), BF),
        ((total, 4 * HD), BF),
        ((total, 4 * HD), BF),
        ((total, HD), F32),
        ((total, HD), F32),
        ((HK, 4 * nz, 16, HD), BF),
        ((HK, 4 * nz, 16, HD), F32),
        ((HK, 2 * nz, 16, HD), BF),
        ((HK, nz, 16, HD), BF),
        ((HK, nz, 16, HD), F32),
        ((HK, nz, 16, HD), BF),
        ((HK, nz, 16, HD), BF),
        ((HK, nz, 16, HD), F32),
        ((HK, nz - 1, 16, HD), BF),
        ((HK, 2, 2 * HD, HD), BF),
        ((HK, 2, 2 * HD, HD), F32),
        ((HK, 2 * HD, HD), BF),
        ((HK, 2 * HD, HD), BF),
        ((HK, 2 * HD, HD), BF),
        ((HK, 2 * HD, HD), BF),
    ]
    shapes = [
        jax.ShapeDtypeStruct((rows, flat), BF),
        jax.ShapeDtypeStruct((rows, HK * HD), F32),
        jax.ShapeDtypeStruct((rows, HK * HD), F32),
        jax.ShapeDtypeStruct((8, HK * HD), F32),
        jax.ShapeDtypeStruct((8, HK * HD), F32),
    ]
    results = pl.pallas_call(
        lambda *refs: body(nz, *refs),
        out_shape=shapes,
        in_specs=[whole] + [vmem] * 4 + [whole, vmem],
        out_specs=[whole] + [vmem] * 4,
        scratch_shapes=[pltpu.VMEM(shape, kind) for shape, kind in scratch]
        + [
            pltpu.SemaphoreType.DMA((HK, 3)),
            pltpu.SemaphoreType.DMA((HK, 4)),
            pltpu.SemaphoreType.DMA((1,)),
            pltpu.SemaphoreType.DMA((nz,)),
            pltpu.SemaphoreType.DMA((8, HK)),
            pltpu.SemaphoreType.DMA((8, HK)),
            pltpu.SemaphoreType.DMA((2,)),
            pltpu.SemaphoreType.DMA((quads,)),
        ],
        compiler_params=pltpu.CompilerParams(
            collective_id=0, has_side_effects=True, vmem_limit_bytes=60 * 1024 * 1024
        ),
        cost_estimate=pl.CostEstimate(
            flops=6 * 10**9, bytes_accessed=6 * 10**6, transcendentals=4 * 10**6
        ),
        name="attention_backward",
    )(
        queries,
        resp_key,
        resp_value,
        prompt_key,
        prompt_value,
        out_grad,
        segment.reshape(1, rows),
    )
    return tuple(
        pl.pallas_call(
            hand_over,
            out_shape=shapes,
            in_specs=[vmem] * 5,
            out_specs=[whole] * 5,
            scratch_shapes=[pltpu.SemaphoreType.DMA((5,))],
            cost_estimate=pl.CostEstimate(
                flops=0, bytes_accessed=3 * 10**6, transcendentals=0
            ),
            name="hand_over",
        )(*results)
    )


def solution(mesh):
    spec = P(("grp", "seq"), None)
    return jax.shard_map(
        on_device,
        mesh=mesh,
        in_specs=(spec,) * 6 + (P(("grp", "seq")),),
        out_specs=(spec,) * 5,
        check_vma=False,
    )
```

time: 91.4 us -> 83.4 us (0.912)
  local copies, waits for them, and re-layouts: 5.42 us -> 0 us
  Pallas kernels: 83.6 us -> 81.1 us
    unnamed x13 -> x0, local copies, waits for them, and re-layouts: 5.42 us -> none
    pallas_call x1 -> x2, Pallas kernels: 83.6 us -> 81.1 us  [the longest x1 78.6 us: on_device(): pl.pallas_call(lambda *refs: body(nz, *refs), out_shape=shapes, in_specs=...]
where the time goes in v2:
time: 83.4 us; the launch traced here: 81.8 us
  Pallas kernels  81.1 us (97%)
    pallas_call x1, Pallas kernels, on_device(): pl.pallas_call(lambda *refs: body(nz, *refs), out_shape=shapes, in_specs=...  78.6 us
    pallas_call x1, Pallas kernels, on_device(): pl.pallas_call(hand_over, out_shape=shapes, in_specs=[vmem] * 5, out_spec...  2.55 us

profile of v2, /device:TPU:24, one launch (start us, length us, event | category | flops | bytes accessed | tf_op | source)
XLA Modules:
  0.0 81.8 jit_solution(14253521322485516269)
XLA Ops:
  0.6 78.6 %attention_backward.1 = (bf16[128,4096]{1,0:T(8,128)(2,1)}, f32[128,512]{1,0:T(8,128)}, f32[128,512]{1,0:T(8,128)}, f32[8,512]{1,0:T(8,128)}, f32[8,512]{1,0:T(8,128)}) custom-call(bf16[128,4096]{1,0:T(8,128)(2,1)} %refs_0_.1, bf16[128,512]{1,0:T(8,128)(2,1)} %refs_1_.1, bf16[128,512]{1,0:T(8,128)(2,1)} %refs_2_.1, bf16[8,512]{1,0:T(8,128)(2,1)} %refs_3_.1, ...), custom_call_target="tpu_custom_call" | custom-call | flops 6000000000 | bytes 6000000 | tf_op jit(solution)/shard_map/attention_backward/pallas_call | solution.py:639
  79.2 2.5 %hand_over.1 = (bf16[128,4096]{1,0:T(8,128)(2,1)}, f32[128,512]{1,0:T(8,128)}, f32[128,512]{1,0:T(8,128)}, f32[8,512]{1,0:T(8,128)}, f32[8,512]{1,0:T(8,128)}) custom-call(bf16[128,4096]{1,0:T(8,128)(2,1)} %get-tuple-element.10.refs_0_, f32[128,512]{1,0:T(8,128)} %get-tuple-element.11.refs_1_, f32[128,512]{1,0:T(8,128)} %get-tuple-element.12.refs_2_, ...), custom_call_target="tpu_custom_call" | custom-call | bytes 3000000 | tf_op jit(solution)/shard_map/hand_over/pallas_call | solution.py:672

commit v3 on v2

v3 whole, which is shorter than its diff:
```python
import jax
import jax.numpy as jnp
from jax import lax
from jax.experimental import pallas as pl
from jax.experimental.pallas import tpu as pltpu
from jax.sharding import PartitionSpec as P

MESH = pl.DeviceIdType.MESH
HD = 128
HK = 4
GROUP = 8
PAIRS = GROUP // 2
SCALE = HD ** (-0.5)
BF = jnp.bfloat16
F32 = jnp.float32


def gather_body(
    nz, rk_ref, rv_ref, pk_ref, pv_ref, seg_ref, win, gat, s_kv, r_kv, s_ring, r_ring, s_one, r_one
):
    n = 4 * nz
    keys = 4 * HD
    npr = 32 * nz
    total = keys + npr
    me = lax.axis_index("seq")
    grp = lax.axis_index("grp")
    core = lax.rem(me, 2)
    x = lax.rem(lax.div(me, 2), 2)
    z = lax.div(me, 4)
    peer = me + 1 - 2 * core
    xpeer = me + 2 - 4 * x

    def zpeer(d):
        return lax.rem(me + 4 * d, n)

    def device(index):
        return (grp, index)

    def copy(src, dst, kind, g, to):
        return pltpu.make_async_remote_copy(
            src_ref=src,
            dst_ref=dst,
            send_sem=s_one.at[kind, g],
            recv_sem=r_one.at[kind, g],
            device_id=device(to),
            device_id_type=MESH,
        )

    barrier = pltpu.get_barrier_semaphore()

    def greet(to):
        pl.semaphore_signal(barrier, inc=1, device_id=device(to), device_id_type=MESH)

    greet(peer)
    greet(xpeer)
    greet(lax.rem(me + 2, n))
    greet(lax.rem(me + n - 2, n))
    greet(lax.rem(me + n + 6 * core - 3, n))

    for d in (1, 2, nz - 1, nz - 2):
        greet(zpeer(d))

    labels = jnp.broadcast_to((seg_ref[...] + 1).astype(F32), (16, HD)).astype(BF)
    for g in range(HK):
        cols = slice(g * HD, (g + 1) * HD)
        win[g, 0, 0:HD, :] = rk_ref[:, cols]
        win[g, 0, HD : 2 * HD, :] = rv_ref[:, cols]
        win[g, 0, 2 * HD : 2 * HD + 16, :] = labels
        gat[core, x, z, g] = jnp.concatenate(
            (pk_ref[:, cols].astype(F32), pv_ref[:, cols].astype(F32)), axis=0
        ).astype(BF)
    pl.semaphore_wait(barrier, 9)
    GX, GC = range(2)

    def kv_copy(g, which, from_slot, to_slot, to):
        return pltpu.make_async_remote_copy(
            src_ref=win.at[g, from_slot],
            dst_ref=win.at[g, to_slot],
            send_sem=s_kv.at[g, which],
            recv_sem=r_kv.at[g, to_slot],
            device_id=device(to),
            device_id_type=MESH,
        )

    def kv_far(g):
        return kv_copy(g, 0, 0, 2, lax.rem(me + 2, n))

    def kv_side(g):
        return kv_copy(g, 1, 0, 1 + 2 * core, lax.rem(me + 1 + 2 * core, n))

    def kv_pass(g):
        return kv_copy(g, 2, 2, 3 - 2 * core, peer)

    def kv_forward(g):
        kv_far(g).wait_recv()
        kv_pass(g).start()

    def kv_ready(g):
        kv_copy(g, 1, 0, 1, peer).wait_recv()
        kv_copy(g, 1, 0, 3, peer).wait_recv()

    steps = nz // 4

    def ring_copy(owner, to, d):
        part = gat.at[core, x, owner]
        return pltpu.make_async_remote_copy(
            src_ref=part,
            dst_ref=part,
            send_sem=s_ring.at[0],
            recv_sem=r_ring.at[d],
            device_id=device(to),
            device_id_type=MESH,
        )

    def ring_wait(d):
        ring_copy(lax.rem(z + nz - d, nz), peer, d).wait_recv()

    def ring_step(k):
        if k > 1:
            ring_wait(2 * (k - 1))
            ring_wait(nz - 2 * (k - 1))
        up = lax.rem(z + nz - 2 * (k - 1), nz)
        down = lax.rem(z + 2 * (k - 1), nz)
        ring_copy(up, zpeer(2), 2 * k).start()
        if k < steps:
            ring_copy(down, zpeer(nz - 2), nz - 2 * k).start()
        ring_copy(up, zpeer(1), 2 * k - 1).start()
        ring_copy(down, zpeer(nz - 1), nz - 2 * k + 1).start()

    def gx_copy(g):
        part = gat.at[core, x, pl.ds(0, nz), g]
        return copy(part, part, GX, g, xpeer)

    def gc_copy(g):
        part = gat.at[core, pl.ds(0, 2), pl.ds(0, nz), g]
        return copy(part, part, GC, g, peer)

    def ring_end():
        for k in range(1, steps + 1):
            ring_wait(2 * k - 1)
            ring_wait(nz - 2 * k + 1)
        ring_wait(2 * steps)

    def kv_send(g):
        kv_far(g).start()
        kv_side(g).start()

    kv_send(0)
    ring_step(1)
    for g in range(1, HK):
        kv_send(g)
    kv_forward(0)
    ring_step(2)
    kv_forward(1)
    ring_step(3)
    kv_forward(2)
    ring_step(4)
    kv_forward(3)
    ring_end()
    for g in range(HK):
        gx_copy(g).start()
    for g in range(HK):
        gx_copy(g).wait_recv()
        gc_copy(g).start()
    for g in range(HK):
        kv_ready(g)
    for g in range(HK):
        gc_copy(g).wait_recv()
    sent = gat.at[0, 0, pl.ds(0, nz - 1)]
    pltpu.make_async_remote_copy(
        src_ref=sent,
        dst_ref=sent,
        send_sem=s_ring.at[0],
        recv_sem=r_ring.at[0],
        device_id=device(peer),
        device_id_type=MESH,
    ).wait_send()
    for g in range(HK):
        for one in (kv_far, kv_side, kv_pass, gx_copy, gc_copy):
            one(g).wait_send()


def compute_body(
    nz,
    q_hbm,
    do_hbm,
    win,
    gat,
    dq_hbm,
    pf,
    tf,
    q_ref,
    do_ref,
    dq_ref,
    qt,
    dot,
    bias,
    pr_a,
    pr_b,
    dpr_a,
    dpr_b,
    mr,
    lr,
    sp_a,
    sp_b,
    dpp_a,
    dpp_b,
    kp,
    vp,
    kt,
    pt,
    dst,
    dk_acc,
    dv_acc,
    s_in,
    s_out,
):
    keys = 4 * HD
    npr = 32 * nz
    total = keys + npr
    quads = 2 * HK
    wide = 4 * HD
    me = lax.axis_index("seq")
    q_in = pltpu.make_async_copy(q_hbm, q_ref, s_in.at[0])
    do_in = pltpu.make_async_copy(do_hbm, do_ref, s_in.at[1])
    q_in.start()
    do_in.start()
    q_in.wait()
    do_in.wait()

    def flip(h, carry):
        for i in range(4):
            cols = pl.ds(pl.multiple_of((h * 4 + i) * HD, HD), HD)
            qt[:, cols] = q_ref[:, cols].T
            dot[:, cols] = do_ref[:, cols].T
        return carry

    lax.fori_loop(0, HK * GROUP // 4, flip, 0)

    def make_bias():
        mine = jnp.broadcast_to(win[0, 0, 2 * HD : 2 * HD + 16, :].astype(F32)[0:1], (HD, HD))
        row = lax.broadcasted_iota(jnp.int32, (HD, HD), 1)
        col = lax.broadcasted_iota(jnp.int32, (HD, HD), 0)
        for slot in range(4):
            theirs = jnp.broadcast_to(
                win[0, slot, 2 * HD : 2 * HD + 16, :].astype(F32)[0:1], (HD, HD)
            ).T
            seen = mine == theirs
            if slot == 0:
                seen = seen & (col <= row)
            else:
                seen = seen & (jnp.broadcast_to(me, (HD, HD)) >= slot)
            bias[slot] = jnp.where(seen, 0.0, -jnp.inf)

    def fold(value, op):
        return op(value.reshape(value.shape[0] // 8, 8, value.shape[1]), axis=0)

    def half_cols(quad, half):
        return pl.ds(pl.multiple_of(quad * wide + half * 2 * HD, 2 * HD), 2 * HD)

    def quad_cols(quad):
        return pl.ds(pl.multiple_of(quad * wide, wide), wide)

    def resp_half(quad, half, pr, dpr):
        g = lax.div(quad, 2)
        cols = half_cols(quad, half)
        k4 = win[g, :, 0:HD, :].reshape(keys, HD)
        v4 = win[g, :, HD : 2 * HD, :].reshape(keys, HD)
        scores = jnp.dot(k4, qt[:, cols], preferred_element_type=F32)
        high = None
        for slot in range(4):
            mask = bias[slot]
            part = scores[slot * HD : (slot + 1) * HD] + jnp.concatenate((mask, mask), axis=1)
            pr[quad, slot] = part
            top = fold(part, jnp.max)
            high = top if high is None else jnp.maximum(high, top)
        high = jnp.max(high, axis=0, keepdims=True)
        dpr[quad] = jnp.dot(v4, dot[:, cols], preferred_element_type=F32).reshape(4, HD, 2 * HD)
        low = None
        for slot in range(4):
            part = jnp.exp((pr[quad, slot] - high) * SCALE)
            pr[quad, slot] = part
            add = fold(part, jnp.sum)
            low = add if low is None else low + add
        mr[quad, half] = jnp.broadcast_to(high, (8, 2 * HD))
        lr[quad, half] = jnp.broadcast_to(jnp.sum(low, axis=0, keepdims=True), (8, 2 * HD))

    def prompt_ready(g):
        all_rows = gat[:, :, :, g].reshape(4 * nz, 16, HD).astype(F32)
        kp[g] = all_rows[:, 0:8].reshape(npr, HD).astype(BF)
        vp[g] = all_rows[:, 8:16].reshape(npr, HD).astype(BF)
        for slot in range(4):
            kt[g, :, slot * HD : (slot + 1) * HD] = win[g, slot, 0:HD, :].T
        for lower in range(0, npr, HD):
            kt[g, :, keys + lower : keys + lower + HD] = kp[g, lower : lower + HD, :].T

    chunks = npr // HD

    def full_half(quad, half, pr, dpr, sp, dpp):
        g = lax.div(quad, 2)
        cols = half_cols(quad, half)
        own = slice(half * 2 * HD, (half + 1) * 2 * HD)
        scores = jnp.dot(kp[g], qt[:, cols], preferred_element_type=F32)
        sp[...] = scores
        high = jnp.maximum(mr[quad, half], fold(scores, jnp.max))
        dpp[...] = jnp.dot(vp[g], dot[:, cols], preferred_element_type=F32)
        old = mr[quad, half][0:1]
        high = jnp.max(high, axis=0, keepdims=True)
        low = None
        for c in range(chunks):
            rows = slice(c * HD, (c + 1) * HD)
            part = jnp.exp((sp[rows, :] - high) * SCALE)
            sp[rows, :] = part
            add = fold(part, jnp.sum)
            low = add if low is None else low + add
        shrink = jnp.exp((old - high) * SCALE)
        sums = jnp.sum(low, axis=0, keepdims=True) + lr[quad, half][0:1] * shrink
        f_prompt = 1.0 / sums
        f_resp = shrink * f_prompt
        delta = None
        for slot in range(4):
            rounded = (pr[quad, slot] * f_resp).astype(BF)
            pt[slot * HD : (slot + 1) * HD, own] = rounded
            add = fold(rounded.astype(F32) * dpr[quad, slot], jnp.sum)
            delta = add if delta is None else delta + add
        for c in range(chunks):
            rows = slice(c * HD, (c + 1) * HD)
            rounded = (sp[rows, :] * f_prompt).astype(BF)
            pt[keys + c * HD : keys + (c + 1) * HD, own] = rounded
            delta = delta + fold(rounded.astype(F32) * dpp[rows, :], jnp.sum)
        delta = jnp.sum(delta, axis=0, keepdims=True)
        for slot in range(4):
            dst[slot * HD : (slot + 1) * HD, own] = (
                (pr[quad, slot] * f_resp) * (dpr[quad, slot] - delta)
            ).astype(BF)
        for c in range(chunks):
            rows = slice(c * HD, (c + 1) * HD)
            dst[keys + c * HD : keys + (c + 1) * HD, own] = (
                (sp[rows, :] * f_prompt) * (dpp[rows, :] - delta)
            ).astype(BF)

    def full_quad(quad):
        full_half(quad, 0, pr_a, dpr_a, sp_a, dpp_a)
        full_half(quad, 1, pr_b, dpr_b, sp_b, dpp_b)

    def rows_of(ref, quad):
        part = ref[:, quad_cols(quad)]
        return jnp.concatenate([part[:, i * HD : (i + 1) * HD] for i in range(4)], axis=0)

    def add_keys(quad, lower, upper):
        second = lax.rem(quad, 2) == 1
        rows = slice(lower, upper)
        for acc, left, right in ((dv_acc, pt, do_ref), (dk_acc, dst, q_ref)):
            part = jnp.dot(left[rows, :], rows_of(right, quad), preferred_element_type=F32)
            acc[rows, :] = jnp.where(second, acc[rows, :], 0.0) + part

    def query_part(quad):
        g = lax.div(quad, 2)
        part = jnp.dot(kt[g], dst[...], preferred_element_type=F32)
        dq_ref[:, quad_cols(quad)] = jnp.concatenate(
            [(part[:, i * HD : (i + 1) * HD].T * SCALE).astype(BF) for i in range(4)], axis=1
        )

    def query_out(quad):
        cols = quad_cols(quad)
        return pltpu.make_async_copy(dq_ref.at[:, cols], dq_hbm.at[:, cols], s_out.at[quad])

    def emit(g):
        dk = dk_acc[keys:total, :] * SCALE
        dv = dv_acc[keys:total, :]
        pf[g] = jnp.concatenate(
            (dk.reshape(4 * nz, 8, HD), dv.reshape(4 * nz, 8, HD)), axis=1
        )
        for slot in range(4):
            rows = slice(slot * HD, (slot + 1) * HD)
            tf[g, slot, 0:HD, :] = dk_acc[rows, :] * SCALE
            tf[g, slot, HD : 2 * HD, :] = dv_acc[rows, :]

    def resp_quad(quad):
        resp_half(quad, 0, pr_a, dpr_a)
        resp_half(quad, 1, pr_b, dpr_b)

    make_bias()
    for g in range(HK):
        prompt_ready(g)
    resp_quad(0)
    resp_quad(1)
    full_quad(0)

    def both_step(quad, carry):
        add_keys(quad - 2, 0, total)
        query_part(quad - 2)
        resp_quad(quad)
        full_quad(quad - 1)
        query_out(quad - 2).start()

        @pl.when(lax.rem(quad, 2) == 1)
        def _():
            emit(lax.div(quad - 2, 2))

        return carry

    lax.fori_loop(2, quads, both_step, 0)
    add_keys(quads - 2, 0, total)
    query_part(quads - 2)
    full_quad(quads - 1)
    query_out(quads - 2).start()
    add_keys(quads - 1, 0, total)
    query_part(quads - 1)
    query_out(quads - 1).start()
    emit(HK - 1)
    for quad in range(quads):
        query_out(quad).wait()


def reduce_body(
    nz,
    pf,
    tf,
    drk_ref,
    drv_ref,
    dpk_ref,
    dpv_ref,
    ps,
    rc,
    xs,
    xf,
    rx,
    zs,
    zf,
    rz,
    ry,
    ys,
    tb,
    rp,
    ts,
    ra,
    rb,
    s_one,
    r_one,
):
    n = 4 * nz
    keys = 4 * HD
    npr = 32 * nz
    total = keys + npr
    me = lax.axis_index("seq")
    grp = lax.axis_index("grp")
    core = lax.rem(me, 2)
    x = lax.rem(lax.div(me, 2), 2)
    z = lax.div(me, 4)
    peer = me + 1 - 2 * core
    xpeer = me + 2 - 4 * x

    def zpeer(d):
        return lax.rem(me + 4 * d, n)

    def device(index):
        return (grp, index)

    def copy(src, dst, kind, g, to):
        return pltpu.make_async_remote_copy(
            src_ref=src,
            dst_ref=dst,
            send_sem=s_one.at[kind, g],
            recv_sem=r_one.at[kind, g],
            device_id=device(to),
            device_id_type=MESH,
        )

    barrier = pltpu.get_barrier_semaphore()

    def greet(to):
        pl.semaphore_signal(barrier, inc=1, device_id=device(to), device_id_type=MESH)

    greet(peer)
    greet(xpeer)
    greet(lax.rem(me + 2, n))
    greet(lax.rem(me + n - 2, n))
    greet(lax.rem(me + n + 6 * core - 3, n))

    for d in range(1, 5):
        greet(zpeer(d))
        greet(zpeer(nz - d))
    PC, PX, PZ, PY, PW, TP, TB, TA = range(8)
    half_blocks = 2 * nz
    for g in range(HK):
        ps[g] = pf[g, pl.ds((1 - core) * half_blocks, half_blocks)].astype(BF)
        for i in range(2):
            tb[g, i] = tf[g, 2 * i + 1].astype(BF)
    pl.semaphore_wait(barrier, 13)

    def pc_copy(g):
        return copy(ps.at[g], rc.at[g], PC, g, peer)

    def px_copy(g):
        return copy(xs.at[g], rx.at[g], PX, g, xpeer)

    def px_send(g):
        pc_copy(g).wait_recv()
        away = 1 - x
        xs[g] = (
            pf[g, pl.ds(core * half_blocks + away * nz, nz)]
            + rc[g, pl.ds(away * nz, nz)].astype(F32)
        ).astype(BF)
        xf[g] = (
            pf[g, pl.ds(core * half_blocks + x * nz, nz)] + rc[g, pl.ds(x * nz, nz)].astype(F32)
        )
        px_copy(g).start()

    def near(g, d, slot):
        return copy(zs.at[g, lax.rem(z + d, nz)], rz.at[g, slot], PZ, g, zpeer(d))

    def far(g, d, by, slot):
        return copy(zs.at[g, lax.rem(z + d, nz)], ry.at[g, slot], PY, g, zpeer(by))

    def relay(g, d, slot):
        return copy(ys.at[g, slot], rz.at[g, 6 + slot], PW, g, zpeer(d))

    def pz_send(g):
        px_copy(g).wait_recv()
        sums = xf[g] + rx[g].astype(F32)
        zf[g] = sums
        zs[g] = sums.astype(BF)
        for k in range(1, 5):
            far(g, nz - 4 - k, nz - k, k - 1).start()
        for k in range(1, 4):
            far(g, 4 + k, k, 3 + k).start()
        for k in range(1, 4):
            near(g, k, k - 1).start()
            near(g, nz - k, 2 + k).start()

    def far_all(g):
        return copy(zs.at[g, pl.ds(0, 7)], ry.at[g], PY, g, peer)

    def near_all(g):
        return copy(zs.at[g, pl.ds(0, 6)], rz.at[g, pl.ds(0, 6)], PZ, g, peer)

    def relay_all(g):
        return copy(ys.at[g], rz.at[g, pl.ds(6, 2)], PW, g, peer)

    def pw_send(g):
        far_all(g).wait_recv()
        below = zf[g, lax.rem(z + nz - 4, nz)] + jnp.sum(ry[g, 0:4].astype(F32), axis=0)
        above = zf[g, lax.rem(z + 4, nz)] + jnp.sum(ry[g, 4:7].astype(F32), axis=0)
        ys[g, 0] = below.astype(BF)
        ys[g, 1] = above.astype(BF)
        relay(g, nz - 4, 0).start()
        relay(g, 4, 1).start()

    def prompt_out(g):
        near_all(g).wait_recv()
        relay_all(g).wait_recv()
        sums = zf[g, z] + jnp.sum(rz[g].astype(F32), axis=0)
        cols = slice(g * HD, (g + 1) * HD)
        dpk_ref[:, cols] = sums[0:8]
        dpv_ref[:, cols] = sums[8:16]

    def tp_copy(g):
        return copy(tb.at[g, core], rp.at[g], TP, g, peer)

    def tb_copy(g):
        return copy(tb.at[g, 1 - core], rb.at[g], TB, g, lax.rem(me + n - 3 + 2 * core, n))

    def ta_copy(g):
        return copy(ts.at[g], ra.at[g], TA, g, lax.rem(me + n - 2, n))

    def ts_send(g):
        tp_copy(g).wait_recv()
        ts[g] = (tf[g, 2] + rp[g].astype(F32)).astype(BF)
        ta_copy(g).start()

    def resp_out(g):
        ta_copy(g).wait_recv()
        tb_copy(g).wait_recv()
        sums = tf[g, 0] + ra[g].astype(F32) + rb[g].astype(F32)
        cols = slice(g * HD, (g + 1) * HD)
        drk_ref[:, cols] = sums[0:HD]
        drv_ref[:, cols] = sums[HD : 2 * HD]

    for g in range(HK):
        pc_copy(g).start()
        tp_copy(g).start()
    for g in range(HK):
        px_send(g)
        ts_send(g)
        tb_copy(g).start()
    for g in range(HK):
        pz_send(g)
    for g in range(HK):
        pw_send(g)
    for g in range(HK):
        resp_out(g)
        prompt_out(g)
    for g in range(HK):
        for one in (pc_copy, px_copy, near_all, far_all, relay_all, tp_copy, tb_copy, ta_copy):
            one(g).wait_send()


def hand_over(*refs):
    sems = refs[8]
    copies = [pltpu.make_async_copy(refs[i], refs[4 + i], sems.at[i]) for i in range(4)]
    for one in copies:
        one.start()
    for one in copies:
        one.wait()


def on_device(queries, resp_key, resp_value, prompt_key, prompt_value, out_grad, segment):
    n = lax.axis_size("seq")
    nz = n // 4
    rows = queries.shape[0]
    npr = 32 * nz
    total = 4 * HD + npr
    quads = 2 * HK
    flat = HK * GROUP * HD
    vmem = pl.BlockSpec(memory_space=pltpu.VMEM)
    whole = pl.BlockSpec(memory_space=pl.ANY)
    shape = jax.ShapeDtypeStruct

    def space(*pieces):
        return [pltpu.VMEM(dims, kind) for dims, kind in pieces]

    def dma(*dims):
        return pltpu.SemaphoreType.DMA(dims)

    win, gat = pl.pallas_call(
        lambda *refs: gather_body(nz, *refs),
        out_shape=[
            shape((HK, 4, 2 * HD + 16, HD), BF),
            shape((2, 2, nz, HK, 16, HD), BF),
        ],
        in_specs=[vmem] * 5,
        out_specs=[vmem] * 2,
        scratch_shapes=[dma(HK, 3), dma(HK, 4), dma(1), dma(nz), dma(2, HK), dma(2, HK)],
        compiler_params=pltpu.CompilerParams(
            collective_id=0, has_side_effects=True, vmem_limit_bytes=32 * 1024 * 1024
        ),
        name="gather",
    )(resp_key, resp_value, prompt_key, prompt_value, segment.reshape(1, rows))
    dq, pf, tf = pl.pallas_call(
        lambda *refs: compute_body(nz, *refs),
        out_shape=[
            shape((rows, flat), BF),
            shape((HK, 4 * nz, 16, HD), F32),
            shape((HK, 4, 2 * HD, HD), F32),
        ],
        in_specs=[whole, whole, vmem, vmem],
        out_specs=[whole, vmem, vmem],
        scratch_shapes=space(
            ((rows, flat), BF),
            ((rows, flat), BF),
            ((rows, flat), BF),
            ((HD, flat), BF),
            ((HD, flat), BF),
            ((4, HD, HD), F32),
            ((quads, 4, HD, 2 * HD), F32),
            ((quads, 4, HD, 2 * HD), F32),
            ((quads, 4, HD, 2 * HD), F32),
            ((quads, 4, HD, 2 * HD), F32),
            ((quads, 2, 8, 2 * HD), F32),
            ((quads, 2, 8, 2 * HD), F32),
            ((npr, 2 * HD), F32),
            ((npr, 2 * HD), F32),
            ((npr, 2 * HD), F32),
            ((npr, 2 * HD), F32),
            ((HK, npr, HD), BF),
            ((HK, npr, HD), BF),
            ((HK, HD, total), BF),
            ((total, 4 * HD), BF),
            ((total, 4 * HD), BF),
            ((total, HD), F32),
            ((total, HD), F32),
        )
        + [dma(2), dma(quads)],
        compiler_params=pltpu.CompilerParams(vmem_limit_bytes=56 * 1024 * 1024),
        name="attention_backward",
    )(queries, out_grad, win, gat)
    results = pl.pallas_call(
        lambda *refs: reduce_body(nz, *refs),
        out_shape=[
            shape((rows, HK * HD), F32),
            shape((rows, HK * HD), F32),
            shape((8, HK * HD), F32),
            shape((8, HK * HD), F32),
        ],
        in_specs=[vmem] * 2,
        out_specs=[vmem] * 4,
        scratch_shapes=space(
            ((HK, 2 * nz, 16, HD), BF),
            ((HK, 2 * nz, 16, HD), BF),
            ((HK, nz, 16, HD), BF),
            ((HK, nz, 16, HD), F32),
            ((HK, nz, 16, HD), BF),
            ((HK, nz, 16, HD), BF),
            ((HK, nz, 16, HD), F32),
            ((HK, 8, 16, HD), BF),
            ((HK, 7, 16, HD), BF),
            ((HK, 2, 16, HD), BF),
            ((HK, 2, 2 * HD, HD), BF),
            ((HK, 2 * HD, HD), BF),
            ((HK, 2 * HD, HD), BF),
            ((HK, 2 * HD, HD), BF),
            ((HK, 2 * HD, HD), BF),
        )
        + [dma(8, HK), dma(8, HK)],
        compiler_params=pltpu.CompilerParams(
            collective_id=1, has_side_effects=True, vmem_limit_bytes=32 * 1024 * 1024
        ),
        name="reduce",
    )(pf, tf)
    handed = pl.pallas_call(
        hand_over,
        out_shape=[shape(r.shape, r.dtype) for r in results],
        in_specs=[vmem] * 4,
        out_specs=[whole] * 4,
        scratch_shapes=[dma(4)],
        name="hand_over",
    )(*results)
    return (dq, *handed)


def solution(mesh):
    spec = P(("grp", "seq"), None)
    return jax.shard_map(
        on_device,
        mesh=mesh,
        in_specs=(spec,) * 6 + (P(("grp", "seq")),),
        out_specs=(spec,) * 5,
        check_vma=False,
    )
```

time: 83.4 us -> 109 us (1.31)
  Pallas kernels: 81.1 us -> 95.5 us
  local copies, waits for them, and re-layouts: 0 us -> 11.6 us
    pallas_call x2 -> x4, Pallas kernels: 81.1 us -> 95.5 us  [the longest x1 38.6 us: on_device(): pl.pallas_call(lambda *refs: gather_body(nz, *refs), out_shape=[shape((HK...]
    unnamed x0 -> x26, local copies, waits for them, and re-layouts: none -> 11.6 us
where the time goes in v3:
time: 109 us; the launch traced here: 108 us
  Pallas kernels  95.5 us (88%)
  local copies, waits for them, and re-layouts  11.6 us (11%)
    pallas_call x1, Pallas kernels, on_device(): pl.pallas_call(lambda *refs: gather_body(nz, *refs), out_shape=[shape((HK...  38.6 us
    pallas_call x1, Pallas kernels, on_device(): pl.pallas_call(lambda *refs: reduce_body(nz, *refs), out_shape=[shape((ro...  28.3 us
    pallas_call x1, Pallas kernels, on_device(): pl.pallas_call(lambda *refs: compute_body(nz, *refs), out_shape=[shape((r...  26.8 us
    unnamed x26, local copies, waits for them, and re-layouts  11.6 us

profile of v3, /device:TPU:24, one launch (start us, length us, event | category | flops | bytes accessed | tf_op | source)
XLA Modules:
  0.0 107.8 jit_solution(12370369146186265339)
XLA Ops:
  0.6 0.0 copy-start.6
  0.6 0.9 copy-done.6
  1.5 0.0 copy-start.7
  1.5 0.9 copy-done.7
  2.4 0.0 copy-start.10
  2.4 0.7 copy-done.10
  3.1 0.0 copy-start.11
  3.1 0.7 copy-done.11
  3.8 0.0 copy-start.12
  3.8 0.7 copy-done.12
  4.5 38.6 %gather.1 = (bf16[4,4,272,128]{3,2,1,0:T(8,128)(2,1)S(1)}, bf16[2,2,16,4,16,128]{5,4,3,2,1,0:T(8,128)(2,1)S(1)}) custom-call(bf16[128,512]{1,0:T(8,128)(2,1)S(1)} %copy-done.6, bf16[128,512]{1,0:T(8,128)(2,1)S(1)} %copy-done.7, bf16[8,512]{1,0:T(8,128)(2,1)S(1)} %copy-done.10, bf16[8,512]{1,0:T(8,128)(2,1)S(1)} %copy-done.11, s32[1,128]{1,0:T(1,128)S(1)} %bitcast.1), custom_call_target="tpu_custom_call" | custom-call | tf_op jit(solution)/shard_map/gather/pallas_call | solution.py:626
  43.1 0.0 copy-start.2
  43.1 1.0 copy-done.2
  44.1 0.0 copy-start.3
  44.1 1.0 copy-done.3
  45.1 26.8 %attention_backward.1 = (bf16[128,4096]{1,0:T(8,128)(2,1)}, f32[4,64,16,128]{3,2,1,0:T(8,128)}, f32[4,4,256,128]{3,2,1,0:T(8,128)}) custom-call(bf16[128,4096]{1,0:T(8,128)(2,1)} %refs_0_.3, bf16[128,4096]{1,0:T(8,128)(2,1)} %refs_1_.3, bf16[4,4,272,128]{3,2,1,0:T(8,128)(2,1)} %copy-done.2, bf16[2,2,16,4,16,128]{5,4,3,2,1,0:T(8,128)(2,1)} %copy-done.3), custom_call_target="tpu_custom_call" | custom-call | tf_op jit(solution)/shard_map/attention_backward/pallas_call | solution.py:640
  71.9 0.0 copy-start
  71.9 1.6 %copy-done = f32[4,64,16,128]{3,2,1,0:T(8,128)S(1)} copy-done((f32[4,64,16,128]{3,2,1,0:T(8,128)S(1)}, f32[4,64,16,128]{3,2,1,0:T(8,128)}, u32[]{:S(2)}) %copy-start) | copy-done | bytes 2097176
  73.5 0.0 copy-start.1
  73.5 1.6 %copy-done.1 = f32[4,4,256,128]{3,2,1,0:T(8,128)S(1)} copy-done((f32[4,4,256,128]{3,2,1,0:T(8,128)S(1)}, f32[4,4,256,128]{3,2,1,0:T(8,128)}, u32[]{:S(2)}) %copy-start.1) | copy-done | bytes 2097176
  75.1 28.3 %reduce.1 = (f32[128,512]{1,0:T(8,128)S(1)}, f32[128,512]{1,0:T(8,128)S(1)}, f32[8,512]{1,0:T(8,128)S(1)}, f32[8,512]{1,0:T(8,128)S(1)}) custom-call(f32[4,64,16,128]{3,2,1,0:T(8,128)S(1)} %copy-done, f32[4,4,256,128]{3,2,1,0:T(8,128)S(1)} %copy-done.1), custom_call_target="tpu_custom_call" | custom-call | tf_op jit(solution)/shard_map/reduce/pallas_call | solution.py:678
  103.4 0.0 copy-start.4
  103.4 0.7 copy-done.4
  104.1 0.0 copy-start.5
  104.1 0.7 copy-done.5
  104.8 0.0 copy-start.8
  104.8 0.6 copy-done.8
  105.4 0.0 copy-start.9
  105.4 0.6 copy-done.9
  106.0 1.9 %hand_over.1 = (f32[128,512]{1,0:T(8,128)}, f32[128,512]{1,0:T(8,128)}, f32[8,512]{1,0:T(8,128)}, f32[8,512]{1,0:T(8,128)}) custom-call(f32[128,512]{1,0:T(8,128)} %copy-done.4, f32[128,512]{1,0:T(8,128)} %copy-done.5, f32[8,512]{1,0:T(8,128)} %copy-done.8, f32[8,512]{1,0:T(8,128)} %copy-done.9), custom_call_target="tpu_custom_call" | custom-call | tf_op jit(solution)/shard_map/hand_over/pallas_call | solution.py:711
Async XLA Ops:
  0.6 0.9 copy-start.6
  1.5 0.9 copy-start.7
  2.4 0.7 copy-start.10
  3.1 0.7 copy-start.11
  3.8 0.7 copy-start.12
  43.1 1.0 copy-start.2
  44.1 1.0 copy-start.3
  71.9 1.6 %copy-start = (f32[4,64,16,128]{3,2,1,0:T(8,128)S(1)}, f32[4,64,16,128]{3,2,1,0:T(8,128)}, u32[]{:S(2)}) copy-start(f32[4,64,16,128]{3,2,1,0:T(8,128)} %get-tuple-element.21.refs_0_) | copy-start | bytes 6291460
  73.5 1.6 %copy-start.1 = (f32[4,4,256,128]{3,2,1,0:T(8,128)S(1)}, f32[4,4,256,128]{3,2,1,0:T(8,128)}, u32[]{:S(2)}) copy-start(f32[4,4,256,128]{3,2,1,0:T(8,128)} %get-tuple-element.22.refs_1_) | copy-start | bytes 6291460
  103.4 0.7 copy-start.4
  104.1 0.7 copy-start.5
  104.8 0.6 copy-start.8
  105.4 0.6 copy-start.9

commit v4 on v2

--- a/solution.py
+++ b/solution.py
@@ -1,5 +1,3 @@
-import math
-
 import jax
 import jax.numpy as jnp
 from jax import lax
@@ -13,7 +11,6 @@
 GROUP = 8
 PAIRS = GROUP // 2
 SCALE = HD ** (-0.5)
-EXP_SCALE = SCALE * math.log2(math.e)
 BF = jnp.bfloat16
 F32 = jnp.float32
 
@@ -21,17 +18,22 @@
 def body(
     nz,
     q_hbm,
-    rk_ref,
-    rv_ref,
-    pk_ref,
-    pv_ref,
+    rk_hbm,
+    rv_hbm,
+    pk_hbm,
+    pv_hbm,
     do_hbm,
-    seg_ref,
+    seg_hbm,
     dq_hbm,
     drk_ref,
     drv_ref,
     dpk_ref,
     dpv_ref,
+    rk_ref,
+    rv_ref,
+    pk_ref,
+    pv_ref,
+    seg_ref,
     q_ref,
     do_ref,
     dq_ref,
@@ -66,6 +68,8 @@
     zs,
     zf,
     rz,
+    ry,
+    ys,
     tb,
     tf,
     rp,
@@ -101,7 +105,7 @@
     def device(index):
         return (grp, index)
 
-    GX, GC, PC, PX, PZ, TP, TB, TA = range(8)
+    GX, GC, PC, PX, PZ, PY, PW, TP, TB, TA = range(10)
 
     def copy(src, dst, kind, g, to):
         return pltpu.make_async_remote_copy(
@@ -113,6 +117,23 @@
             device_id_type=MESH,
         )
 
+    small = [
+        pltpu.make_async_copy(source, target, s_in.at[2 + i])
+        for i, (source, target) in enumerate(
+            (
+                (rk_hbm, rk_ref),
+                (rv_hbm, rv_ref),
+                (pk_hbm, pk_ref),
+                (pv_hbm, pv_ref),
+                (seg_hbm, seg_ref),
+            )
+        )
+    ]
+    q_in = pltpu.make_async_copy(q_hbm, q_ref, s_in.at[0])
+    do_in = pltpu.make_async_copy(do_hbm, do_ref, s_in.at[1])
+    for one in (*small, q_in, do_in):
+        one.start()
+
     barrier = pltpu.get_barrier_semaphore()
 
     def greet(to):
@@ -124,15 +145,11 @@
     greet(lax.rem(me + n - 2, n))
     greet(lax.rem(me + n + 6 * core - 3, n))
 
-    def greet_z(d, carry):
+    for d in range(1, 5):
         greet(zpeer(d))
-        return carry
-
-    lax.fori_loop(1, nz, greet_z, 0)
-    q_in = pltpu.make_async_copy(q_hbm, q_ref, s_in.at[0])
-    do_in = pltpu.make_async_copy(do_hbm, do_ref, s_in.at[1])
-    q_in.start()
-    do_in.start()
+        greet(zpeer(nz - d))
+    for one in small:
+        one.wait()
 
     labels = jnp.broadcast_to((seg_ref[...] + 1).astype(F32), (16, HD)).astype(BF)
     for g in range(HK):
@@ -143,7 +160,7 @@
         gat[core, x, z, g] = jnp.concatenate(
             (pk_ref[:, cols].astype(F32), pv_ref[:, cols].astype(F32)), axis=0
         ).astype(BF)
-    pl.semaphore_wait(barrier, 5 + nz - 1)
+    pl.semaphore_wait(barrier, 13)
 
     def kv_copy(g, which, from_slot, to_slot, to):
         return pltpu.make_async_remote_copy(
@@ -227,7 +244,6 @@
 
     kv_send(0)
     ring_step(1)
-    kv_send(1)
 
     q_in.wait()
     do_in.wait()
@@ -240,9 +256,11 @@
         return carry
 
     lax.fori_loop(0, HK * GROUP // 8, flip, 0)
+    kv_send(1)
     ring_step(2)
     lax.fori_loop(HK * GROUP // 8, HK * GROUP // 4, flip, 0)
     kv_forward(0)
+    kv_send(2)
     ring_step(3)
 
     def make_bias():
@@ -286,7 +304,7 @@
         dpr[quad] = jnp.dot(v4, dot[:, cols], preferred_element_type=F32).reshape(4, HD, 2 * HD)
         low = None
         for slot in range(4):
-            part = jnp.exp2((pr[quad, slot] - high) * EXP_SCALE)
+            part = jnp.exp((pr[quad, slot] - high) * SCALE)
             pr[quad, slot] = part
             add = fold(part, jnp.sum)
             low = add if low is None else low + add
@@ -318,11 +336,11 @@
         low = None
         for c in range(chunks):
             rows = slice(c * HD, (c + 1) * HD)
-            part = jnp.exp2((sp[rows, :] - high) * EXP_SCALE)
+            part = jnp.exp((sp[rows, :] - high) * SCALE)
             sp[rows, :] = part
             add = fold(part, jnp.sum)
             low = add if low is None else low + add
-        shrink = jnp.exp2((old - high) * EXP_SCALE)
+        shrink = jnp.exp((old - high) * SCALE)
         sums = jnp.sum(low, axis=0, keepdims=True) + lr[quad, half][0:1] * shrink
         f_prompt = 1.0 / sums
         f_resp = shrink * f_prompt
@@ -339,12 +357,12 @@
             delta = delta + fold(rounded.astype(F32) * dpp[rows, :], jnp.sum)
         delta = jnp.sum(delta, axis=0, keepdims=True)
         for slot in range(4):
-            dst[slot * HD : (slot + 1) * HD, own] = (
+            dst[quad, slot * HD : (slot + 1) * HD, own] = (
                 (pr[quad, slot] * f_resp) * (dpr[quad, slot] - delta)
             ).astype(BF)
         for c in range(chunks):
             rows = slice(c * HD, (c + 1) * HD)
-            dst[keys + c * HD : keys + (c + 1) * HD, own] = (
+            dst[quad, keys + c * HD : keys + (c + 1) * HD, own] = (
                 (sp[rows, :] * f_prompt) * (dpp[rows, :] - delta)
             ).astype(BF)
 
@@ -359,13 +377,13 @@
     def add_keys(quad, lower, upper):
         second = lax.rem(quad, 2) == 1
         rows = slice(lower, upper)
-        for acc, left, right in ((dv_acc, pt, do_ref), (dk_acc, dst, q_ref)):
+        for acc, left, right in ((dv_acc, pt, do_ref), (dk_acc, dst.at[quad], q_ref)):
             part = jnp.dot(left[rows, :], rows_of(right, quad), preferred_element_type=F32)
             acc[rows, :] = jnp.where(second, acc[rows, :], 0.0) + part
 
     def query_part(quad):
         g = lax.div(quad, 2)
-        part = jnp.dot(kt[g], dst[...], preferred_element_type=F32)
+        part = jnp.dot(kt[g], dst[quad], preferred_element_type=F32)
         dq_ref[:, quad_cols(quad)] = jnp.concatenate(
             [(part[:, i * HD : (i + 1) * HD].T * SCALE).astype(BF) for i in range(4)], axis=1
         )
@@ -420,20 +438,49 @@
         )
         px_copy(g).start()
 
+    def near(g, d, slot):
+        return copy(zs.at[g, lax.rem(z + d, nz)], rz.at[g, slot], PZ, g, zpeer(d))
+
+    def far(g, d, by, slot):
+        return copy(zs.at[g, lax.rem(z + d, nz)], ry.at[g, slot], PY, g, zpeer(by))
+
+    def relay(g, d, slot):
+        return copy(ys.at[g, slot], rz.at[g, 6 + slot], PW, g, zpeer(d))
+
     def pz_send(g):
         px_copy(g).wait_recv()
         sums = xf[g] + rx[g].astype(F32)
         zf[g] = sums
         zs[g] = sums.astype(BF)
-
-        for d in range(1, nz):
-            copy(zs.at[g, lax.rem(z + d, nz)], rz.at[g, d - 1], PZ, g, zpeer(d)).start()
-
-    def pz_all(g):
-        return copy(zs.at[g, pl.ds(0, nz - 1)], rz.at[g], PZ, g, peer)
+        for k in range(1, 5):
+            far(g, nz - 4 - k, nz - k, k - 1).start()
+        for k in range(1, 4):
+            far(g, 4 + k, k, 3 + k).start()
+        for k in range(1, 4):
+            near(g, k, k - 1).start()
+            near(g, nz - k, 2 + k).start()
+
+    def far_all(g):
+        return copy(zs.at[g, pl.ds(0, 7)], ry.at[g], PY, g, peer)
+
+    def near_all(g):
+        return copy(zs.at[g, pl.ds(0, 6)], rz.at[g, pl.ds(0, 6)], PZ, g, peer)
+
+    def relay_all(g):
+        return copy(ys.at[g], rz.at[g, pl.ds(6, 2)], PW, g, peer)
+
+    def pw_send(g):
+        far_all(g).wait_recv()
+        below = zf[g, lax.rem(z + nz - 4, nz)] + jnp.sum(ry[g, 0:4].astype(F32), axis=0)
+        above = zf[g, lax.rem(z + 4, nz)] + jnp.sum(ry[g, 4:7].astype(F32), axis=0)
+        ys[g, 0] = below.astype(BF)
+        ys[g, 1] = above.astype(BF)
+        relay(g, nz - 4, 0).start()
+        relay(g, 4, 1).start()
 
     def prompt_out(g):
-        pz_all(g).wait_recv()
+        near_all(g).wait_recv()
+        relay_all(g).wait_recv()
         sums = zf[g, z] + jnp.sum(rz[g].astype(F32), axis=0)
         cols = slice(g * HD, (g + 1) * HD)
         dpk_ref[:, cols] = sums[0:8]
@@ -477,16 +524,16 @@
     def resp_step(quad, carry):
         when(quad == 2, (kv_ready, 1))
         resp_quad(quad)
-        when(quad == 0, (ring_step, 4), (kv_forward, 1))
+        when(quad == 0, (ring_step, 4), (kv_forward, 1), (kv_send, 3))
 
         @pl.when(quad == 1)
         def _():
             ring_end()
-            gather_x(0)
-            kv_send(2)
-
-        when(quad == 2, (gather_x, 1))
-        when(quad == 3, (gather_c, 0), (kv_forward, 2), (kv_send, 3))
+            for g in range(HK):
+                gather_x(g)
+
+        when(quad == 2, (kv_forward, 2))
+        when(quad == 3, (gather_c, 0))
         return carry
 
     lax.fori_loop(0, 4, resp_step, 0)
@@ -495,16 +542,13 @@
     resp_quad(4)
     full_quad(0)
     gather_c(1)
-    gather_x(2)
 
     def both_step(quad, carry):
         when(quad == 6, (kv_ready, 3), (prompt_ready, 1))
         add_keys(quad - 5, 0, total)
-        query_part(quad - 5)
         resp_quad(quad)
         full_quad(quad - 4)
-        query_out(quad - 5).start()
-        when(quad == 5, (kv_forward, 3), (gather_x, 3))
+        when(quad == 5, (kv_forward, 3))
         when(quad == 6, (emit_prompt, 0), (emit_resp, 0), (gather_c, 2))
         when(quad == 7, (gather_c, 3), (px_send, 0), (ts_send, 0))
         return carry
@@ -516,28 +560,36 @@
         first = lax.rem(quad, 2) == 0
         when(first, (prompt_ready, g))
         add_keys(quad - 1, 0, total)
-        query_part(quad - 1)
         full_quad(quad)
-        query_out(quad - 1).start()
         when(first, (emit_prompt, g - 1), (emit_resp, g - 1), (pz_send, g - 2))
-        when(~first, (px_send, g - 1), (ts_send, g - 1))
+        when(~first, (px_send, g - 1), (ts_send, g - 1), (pw_send, g - 2))
         return carry
 
     lax.fori_loop(4, quads, full_step, 0)
+
+    def query(*which):
+        for quad in which:
+            query_part(quad)
+            query_out(quad).start()
+
     last = HK - 1
     add_keys(quads - 1, keys, total)
     emit_prompt(last)
-    pz_send(last - 1)
     add_keys(quads - 1, 0, keys)
     emit_resp(last)
-    query_part(quads - 1)
-    query_out(quads - 1).start()
+    pz_send(last - 1)
+    query(0, 1, 2)
     px_send(last)
     ts_send(last)
+    query(3, 4)
+    pw_send(last - 1)
+    query(5)
+    pz_send(last)
+    query(6, 7)
     for g in range(last):
         prompt_out(g)
         resp_out(g)
-    pz_send(last)
+    pw_send(last)
     resp_out(last)
     prompt_out(last)
 
@@ -558,7 +610,9 @@
         gc_copy(g).wait_send()
         pc_copy(g).wait_send()
         px_copy(g).wait_send()
-        pz_all(g).wait_send()
+        near_all(g).wait_send()
+        far_all(g).wait_send()
+        relay_all(g).wait_send()
         tp_copy(g).wait_send()
         tb_copy(g).wait_send()
         ta_copy(g).wait_send()
@@ -588,6 +642,11 @@
     whole = pl.BlockSpec(memory_space=pl.ANY)
     flat = HK * GROUP * HD
     scratch = [
+        ((rows, HK * HD), BF),
+        ((rows, HK * HD), BF),
+        ((8, HK * HD), BF),
+        ((8, HK * HD), BF),
+        ((1, rows), jnp.int32),
         ((rows, flat), BF),
         ((rows, flat), BF),
         ((rows, flat), BF),
@@ -610,7 +669,7 @@
         ((HK, npr, HD), BF),
         ((HK, HD, total), BF),
         ((total, 4 * HD), BF),
-        ((total, 4 * HD), BF),
+        ((quads, total, 4 * HD), BF),
         ((total, HD), F32),
         ((total, HD), F32),
         ((HK, 4 * nz, 16, HD), BF),
@@ -621,7 +680,9 @@
         ((HK, nz, 16, HD), BF),
         ((HK, nz, 16, HD), BF),
         ((HK, nz, 16, HD), F32),
-        ((HK, nz - 1, 16, HD), BF),
+        ((HK, 8, 16, HD), BF),
+        ((HK, 7, 16, HD), BF),
+        ((HK, 2, 16, HD), BF),
         ((HK, 2, 2 * HD, HD), BF),
         ((HK, 2, 2 * HD, HD), F32),
         ((HK, 2 * HD, HD), BF),
@@ -639,7 +700,7 @@
     results = pl.pallas_call(
         lambda *refs: body(nz, *refs),
         out_shape=shapes,
-        in_specs=[whole] + [vmem] * 4 + [whole, vmem],
+        in_specs=[whole] * 7,
         out_specs=[whole] + [vmem] * 4,
         scratch_shapes=[pltpu.VMEM(shape, kind) for shape, kind in scratch]
         + [
@@ -647,9 +708,9 @@
             pltpu.SemaphoreType.DMA((HK, 4)),
             pltpu.SemaphoreType.DMA((1,)),
             pltpu.SemaphoreType.DMA((nz,)),
-            pltpu.SemaphoreType.DMA((8, HK)),
-            pltpu.SemaphoreType.DMA((8, HK)),
-            pltpu.SemaphoreType.DMA((2,)),
+            pltpu.SemaphoreType.DMA((10, HK)),
+            pltpu.SemaphoreType.DMA((10, HK)),
+            pltpu.SemaphoreType.DMA((7,)),
             pltpu.SemaphoreType.DMA((quads,)),
         ],
         compiler_params=pltpu.CompilerParams(

time: 83.4 us -> 81 us (0.971); the launches traced: 81.8 us -> 80.8 us
  Pallas kernels: 81.1 us -> 80.2 us
    pallas_call x1, Pallas kernels: 78.6 us -> 77.6 us  [on_device(): pl.pallas_call(lambda *refs: body(nz, *refs), out_shape=shapes, in_specs=...]
where the time goes in v4:
time: 81 us; the launch traced here: 80.8 us
  Pallas kernels  80.2 us (99%)
    pallas_call x1, Pallas kernels, on_device(): pl.pallas_call(lambda *refs: body(nz, *refs), out_shape=shapes, in_specs=...  77.6 us
    pallas_call x1, Pallas kernels, on_device(): pl.pallas_call(hand_over, out_shape=shapes, in_specs=[vmem] * 5, out_spec...  2.55 us

profile of v4, /device:TPU:24, one launch (start us, length us, event | category | flops | bytes accessed | tf_op | source)
XLA Modules:
  0.0 80.8 jit_solution(6443904296049678669)
XLA Ops:
  0.6 77.6 %attention_backward.1 = (bf16[128,4096]{1,0:T(8,128)(2,1)}, f32[128,512]{1,0:T(8,128)}, f32[128,512]{1,0:T(8,128)}, f32[8,512]{1,0:T(8,128)}, f32[8,512]{1,0:T(8,128)}) custom-call(bf16[128,4096]{1,0:T(8,128)(2,1)} %refs_0_.1, bf16[128,512]{1,0:T(8,128)(2,1)} %refs_1_.1, bf16[128,512]{1,0:T(8,128)(2,1)} %refs_2_.1, bf16[8,512]{1,0:T(8,128)(2,1)} %refs_3_.1, ...), custom_call_target="tpu_custom_call" | custom-call | flops 6000000000 | bytes 6000000 | tf_op jit(solution)/shard_map/attention_backward/pallas_call | solution.py:700
  78.3 2.5 %hand_over.1 = (bf16[128,4096]{1,0:T(8,128)(2,1)}, f32[128,512]{1,0:T(8,128)}, f32[128,512]{1,0:T(8,128)}, f32[8,512]{1,0:T(8,128)}, f32[8,512]{1,0:T(8,128)}) custom-call(bf16[128,4096]{1,0:T(8,128)(2,1)} %get-tuple-element.10.refs_0_, f32[128,512]{1,0:T(8,128)} %get-tuple-element.11.refs_1_, f32[128,512]{1,0:T(8,128)} %get-tuple-element.12.refs_2_, ...), custom_call_target="tpu_custom_call" | custom-call | bytes 3000000 | tf_op jit(solution)/shard_map/hand_over/pallas_call | solution.py:733

commit v5 on v4

--- a/solution.py
+++ b/solution.py
@@ -105,7 +105,7 @@
     def device(index):
         return (grp, index)
 
-    GX, GC, PC, PX, PZ, PY, PW, TP, TB, TA = range(10)
+    GX, GC, PC, PX, PZ, PY, PW, TP, TB, TA, GZ = range(11)
 
     def copy(src, dst, kind, g, to):
         return pltpu.make_async_remote_copy(
@@ -145,9 +145,8 @@
     greet(lax.rem(me + n - 2, n))
     greet(lax.rem(me + n + 6 * core - 3, n))
 
-    for d in range(1, 5):
+    for d in range(1, nz):
         greet(zpeer(d))
-        greet(zpeer(nz - d))
     for one in small:
         one.wait()
 
@@ -160,7 +159,7 @@
         gat[core, x, z, g] = jnp.concatenate(
             (pk_ref[:, cols].astype(F32), pv_ref[:, cols].astype(F32)), axis=0
         ).astype(BF)
-    pl.semaphore_wait(barrier, 13)
+    pl.semaphore_wait(barrier, 5 + nz - 1)
 
     def kv_copy(g, which, from_slot, to_slot, to):
         return pltpu.make_async_remote_copy(
@@ -192,7 +191,7 @@
     steps = nz // 4
 
     def ring_copy(owner, to, d):
-        part = gat.at[core, x, owner]
+        part = gat.at[core, x, owner, pl.ds(1, HK - 1)]
         return pltpu.make_async_remote_copy(
             src_ref=part,
             dst_ref=part,
@@ -217,6 +216,14 @@
         ring_copy(up, zpeer(1), 2 * k - 1).start()
         ring_copy(down, zpeer(nz - 1), nz - 2 * k + 1).start()
 
+    def gz_copy(d):
+        part = gat.at[core, x, z, 0]
+        return copy(part, part, GZ, 0, zpeer(d))
+
+    def gz_all():
+        part = gat.at[core, x, pl.ds(0, nz - 1), 0]
+        return copy(part, part, GZ, 0, peer)
+
     def gx_copy(g):
         part = gat.at[core, x, pl.ds(0, nz), g]
         return copy(part, part, GX, g, xpeer)
@@ -243,6 +250,10 @@
         kv_side(g).start()
 
     kv_send(0)
+    for d in range(1, nz // 2):
+        gz_copy(nz // 2 - d).start()
+        gz_copy(nz // 2 + d).start()
+    gz_copy(nz // 2).start()
     ring_step(1)
 
     q_in.wait()
@@ -256,12 +267,12 @@
         return carry
 
     lax.fori_loop(0, HK * GROUP // 8, flip, 0)
+    kv_forward(0)
     kv_send(1)
     ring_step(2)
     lax.fori_loop(HK * GROUP // 8, HK * GROUP // 4, flip, 0)
-    kv_forward(0)
-    kv_send(2)
-    ring_step(3)
+    gz_all().wait_recv()
+    gx_copy(0).start()
 
     def make_bias():
         mine = jnp.broadcast_to(win[0, 0, 2 * HD : 2 * HD + 16, :].astype(F32)[0:1], (HD, HD))
@@ -522,38 +533,37 @@
     make_bias()
 
     def resp_step(quad, carry):
-        when(quad == 2, (kv_ready, 1))
         resp_quad(quad)
-        when(quad == 0, (ring_step, 4), (kv_forward, 1), (kv_send, 3))
-
-        @pl.when(quad == 1)
-        def _():
-            ring_end()
-            for g in range(HK):
-                gather_x(g)
-
-        when(quad == 2, (kv_forward, 2))
-        when(quad == 3, (gather_c, 0))
+        when(quad == 0, (ring_step, 3), (kv_forward, 1), (kv_send, 2), (gather_c, 0))
+        when(quad == 1, (ring_step, 4))
         return carry
 
-    lax.fori_loop(0, 4, resp_step, 0)
-    kv_ready(2)
+    lax.fori_loop(0, 2, resp_step, 0)
+    kv_ready(1)
     prompt_ready(0)
-    resp_quad(4)
+    ring_end()
+    for g in range(1, HK):
+        gather_x(g)
+    resp_quad(2)
     full_quad(0)
+    kv_forward(2)
+    kv_send(3)
     gather_c(1)
 
     def both_step(quad, carry):
-        when(quad == 6, (kv_ready, 3), (prompt_ready, 1))
-        add_keys(quad - 5, 0, total)
+        when(quad == 4, (kv_ready, 2), (prompt_ready, 1))
+        when(quad == 6, (kv_ready, 3), (prompt_ready, 2))
+        add_keys(quad - 3, 0, total)
         resp_quad(quad)
-        full_quad(quad - 4)
-        when(quad == 5, (kv_forward, 3))
-        when(quad == 6, (emit_prompt, 0), (emit_resp, 0), (gather_c, 2))
-        when(quad == 7, (gather_c, 3), (px_send, 0), (ts_send, 0))
+        full_quad(quad - 2)
+        when(quad == 3, (gather_c, 2))
+        when(quad == 4, (emit_prompt, 0), (emit_resp, 0), (kv_forward, 3))
+        when(quad == 5, (px_send, 0), (ts_send, 0), (gather_c, 3))
+        when(quad == 6, (emit_prompt, 1), (emit_resp, 1), (pz_send, 0))
+        when(quad == 7, (px_send, 1), (ts_send, 1), (pw_send, 0))
         return carry
 
-    lax.fori_loop(5, quads, both_step, 0)
+    lax.fori_loop(3, quads, both_step, 0)
 
     def full_step(quad, carry):
         g = lax.div(quad, 2)
@@ -565,7 +575,7 @@
         when(~first, (px_send, g - 1), (ts_send, g - 1), (pw_send, g - 2))
         return carry
 
-    lax.fori_loop(4, quads, full_step, 0)
+    lax.fori_loop(quads - 2, quads, full_step, 0)
 
     def query(*which):
         for quad in which:
@@ -593,7 +603,7 @@
     resp_out(last)
     prompt_out(last)
 
-    sent = gat.at[0, 0, pl.ds(0, nz - 1)]
+    sent = gat.at[0, 0, pl.ds(0, nz - 1), pl.ds(1, HK - 1)]
     pltpu.make_async_remote_copy(
         src_ref=sent,
         dst_ref=sent,
@@ -610,6 +620,8 @@
         gc_copy(g).wait_send()
         pc_copy(g).wait_send()
         px_copy(g).wait_send()
+        if g == 0:
+            gz_all().wait_send()
         near_all(g).wait_send()
         far_all(g).wait_send()
         relay_all(g).wait_send()
@@ -708,8 +720,8 @@
             pltpu.SemaphoreType.DMA((HK, 4)),
             pltpu.SemaphoreType.DMA((1,)),
             pltpu.SemaphoreType.DMA((nz,)),
-            pltpu.SemaphoreType.DMA((10, HK)),
-            pltpu.SemaphoreType.DMA((10, HK)),
+            pltpu.SemaphoreType.DMA((11, HK)),
+            pltpu.SemaphoreType.DMA((11, HK)),
             pltpu.SemaphoreType.DMA((7,)),
             pltpu.SemaphoreType.DMA((quads,)),
         ],

time: 81 us -> 83.7 us (1.033)
  Pallas kernels: 80.2 us -> 82.9 us
    pallas_call x1, Pallas kernels: 77.6 us -> 80.4 us  [on_device(): pl.pallas_call(lambda *refs: body(nz, *refs), out_shape=shapes, in_specs=...]
where the time goes in v5:
time: 83.7 us; the launch traced here: 83.6 us
  Pallas kernels  82.9 us (99%)
    pallas_call x1, Pallas kernels, on_device(): pl.pallas_call(lambda *refs: body(nz, *refs), out_shape=shapes, in_specs=...  80.4 us
    pallas_call x1, Pallas kernels, on_device(): pl.pallas_call(hand_over, out_shape=shapes, in_specs=[vmem] * 5, out_spec...  2.55 us

profile of v5, /device:TPU:24, one launch (start us, length us, event | category | flops | bytes accessed | tf_op | source)
XLA Modules:
  0.0 83.6 jit_solution(16090231155325854456)
XLA Ops:
  0.6 80.4 %attention_backward.1 = (bf16[128,4096]{1,0:T(8,128)(2,1)}, f32[128,512]{1,0:T(8,128)}, f32[128,512]{1,0:T(8,128)}, f32[8,512]{1,0:T(8,128)}, f32[8,512]{1,0:T(8,128)}) custom-call(bf16[128,4096]{1,0:T(8,128)(2,1)} %refs_0_.1, bf16[128,512]{1,0:T(8,128)(2,1)} %refs_1_.1, bf16[128,512]{1,0:T(8,128)(2,1)} %refs_2_.1, bf16[8,512]{1,0:T(8,128)(2,1)} %refs_3_.1, ...), custom_call_target="tpu_custom_call" | custom-call | flops 6000000000 | bytes 6000000 | tf_op jit(solution)/shard_map/attention_backward/pallas_call | solution.py:712
  81.0 2.5 %hand_over.1 = (bf16[128,4096]{1,0:T(8,128)(2,1)}, f32[128,512]{1,0:T(8,128)}, f32[128,512]{1,0:T(8,128)}, f32[8,512]{1,0:T(8,128)}, f32[8,512]{1,0:T(8,128)}) custom-call(bf16[128,4096]{1,0:T(8,128)(2,1)} %get-tuple-element.10.refs_0_, f32[128,512]{1,0:T(8,128)} %get-tuple-element.11.refs_1_, f32[128,512]{1,0:T(8,128)} %get-tuple-element.12.refs_2_, ...), custom_call_target="tpu_custom_call" | custom-call | bytes 3000000 | tf_op jit(solution)/shard_map/hand_over/pallas_call | solution.py:745

commit v6 on v4

--- a/solution.py
+++ b/solution.py
@@ -163,9 +163,10 @@
     pl.semaphore_wait(barrier, 13)
 
     def kv_copy(g, which, from_slot, to_slot, to):
+        part = pl.ds(0, 2 * HD + (16 if g == 0 else 0))
         return pltpu.make_async_remote_copy(
-            src_ref=win.at[g, from_slot],
-            dst_ref=win.at[g, to_slot],
+            src_ref=win.at[g, from_slot, part],
+            dst_ref=win.at[g, to_slot, part],
             send_sem=s_kv.at[g, which],
             recv_sem=r_kv.at[g, to_slot],
             device_id=device(to),
@@ -620,15 +621,31 @@
         query_out(quad).wait()
 
 
+PIECES = ((0, 4), (1, 1), (2, 1), (3, 1), (4, 1))
+
+
 def hand_over(*refs):
-    sems = refs[10]
-    copies = [
-        pltpu.make_async_copy(refs[i], refs[5 + i], sems.at[i]) for i in range(5)
-    ]
-    for one in copies:
-        one.start()
-    for one in copies:
-        one.wait()
+    sources, targets, held, sems = refs[:5], refs[5:10], refs[10:15], refs[15]
+    loads, stores = [], []
+    for index, count in PIECES:
+        rows = sources[index].shape[0] // count
+        for i in range(count):
+            part = pl.ds(i * rows, rows)
+            here = held[index].at[part]
+            slot = len(loads)
+            loads.append(
+                pltpu.make_async_copy(sources[index].at[part], here, sems.at[0, slot])
+            )
+            stores.append(
+                pltpu.make_async_copy(here, targets[index].at[part], sems.at[1, slot])
+            )
+    for load in loads:
+        load.start()
+    for load, store in zip(loads, stores):
+        load.wait()
+        store.start()
+    for store in stores:
+        store.wait()
 
 
 def on_device(queries, resp_key, resp_value, prompt_key, prompt_value, out_grad, segment):
@@ -733,9 +750,11 @@
         pl.pallas_call(
             hand_over,
             out_shape=shapes,
-            in_specs=[vmem] * 5,
+            in_specs=[whole] * 5,
             out_specs=[whole] * 5,
-            scratch_shapes=[pltpu.SemaphoreType.DMA((5,))],
+            scratch_shapes=[pltpu.VMEM(one.shape, one.dtype) for one in shapes]
+            + [pltpu.SemaphoreType.DMA((2, sum(count for _, count in PIECES)))],
+            compiler_params=pltpu.CompilerParams(vmem_limit_bytes=60 * 1024 * 1024),
             cost_estimate=pl.CostEstimate(
                 flops=0, bytes_accessed=3 * 10**6, transcendentals=0
             ),

time: 81 us -> 80.5 us (level)
  no operation moved by 1% of the time
where the time goes in v6:
time: 80.5 us; the launch traced here: 80.3 us
  Pallas kernels  79.7 us (99%)
    pallas_call x1, Pallas kernels, on_device(): pl.pallas_call(lambda *refs: body(nz, *refs), out_shape=shapes, in_specs=...  77.5 us
    pallas_call x1, Pallas kernels, on_device(): pl.pallas_call(hand_over, out_shape=shapes, in_specs=[whole] * 5, out_spe...  2.23 us

profile of v6, /device:TPU:24, one launch (start us, length us, event | category | flops | bytes accessed | tf_op | source)
XLA Modules:
  0.0 80.3 jit_solution(11036404602929147499)
XLA Ops:
  0.6 77.5 %attention_backward.1 = (bf16[128,4096]{1,0:T(8,128)(2,1)}, f32[128,512]{1,0:T(8,128)}, f32[128,512]{1,0:T(8,128)}, f32[8,512]{1,0:T(8,128)}, f32[8,512]{1,0:T(8,128)}) custom-call(bf16[128,4096]{1,0:T(8,128)(2,1)} %refs_0_.1, bf16[128,512]{1,0:T(8,128)(2,1)} %refs_1_.1, bf16[128,512]{1,0:T(8,128)(2,1)} %refs_2_.1, bf16[8,512]{1,0:T(8,128)(2,1)} %refs_3_.1, ...), custom_call_target="tpu_custom_call" | custom-call | flops 6000000000 | bytes 6000000 | tf_op jit(solution)/shard_map/attention_backward/pallas_call | solution.py:717
  78.1 2.2 %hand_over.1 = (bf16[128,4096]{1,0:T(8,128)(2,1)}, f32[128,512]{1,0:T(8,128)}, f32[128,512]{1,0:T(8,128)}, f32[8,512]{1,0:T(8,128)}, f32[8,512]{1,0:T(8,128)}) custom-call(bf16[128,4096]{1,0:T(8,128)(2,1)} %get-tuple-element.10.refs_0_, f32[128,512]{1,0:T(8,128)} %get-tuple-element.11.refs_1_, f32[128,512]{1,0:T(8,128)} %get-tuple-element.12.refs_2_, ...), custom_call_target="tpu_custom_call" | custom-call | bytes 3000000 | tf_op jit(solution)/shard_map/hand_over/pallas_call | solution.py:750

commit v7 on v6

--- a/solution.py
+++ b/solution.py
@@ -157,7 +157,7 @@
         win[g, 0, 0:HD, :] = rk_ref[:, cols]
         win[g, 0, HD : 2 * HD, :] = rv_ref[:, cols]
         win[g, 0, 2 * HD : 2 * HD + 16, :] = labels
-        gat[core, x, z, g] = jnp.concatenate(
+        gat[core, x, g, z] = jnp.concatenate(
             (pk_ref[:, cols].astype(F32), pv_ref[:, cols].astype(F32)), axis=0
         ).astype(BF)
     pl.semaphore_wait(barrier, 13)
@@ -193,7 +193,7 @@
     steps = nz // 4
 
     def ring_copy(owner, to, d):
-        part = gat.at[core, x, owner]
+        part = gat.at[core, x, pl.ds(0, HK), owner]
         return pltpu.make_async_remote_copy(
             src_ref=part,
             dst_ref=part,
@@ -219,11 +219,11 @@
         ring_copy(down, zpeer(nz - 1), nz - 2 * k + 1).start()
 
     def gx_copy(g):
-        part = gat.at[core, x, pl.ds(0, nz), g]
+        part = gat.at[core, x, g]
         return copy(part, part, GX, g, xpeer)
 
     def gc_copy(g):
-        part = gat.at[core, pl.ds(0, 2), pl.ds(0, nz), g]
+        part = gat.at[core, pl.ds(0, 2), g]
         return copy(part, part, GC, g, peer)
 
     def ring_end():
@@ -314,7 +314,7 @@
 
     def prompt_ready(g):
         gc_copy(g).wait_recv()
-        all_rows = gat[:, :, :, g].reshape(4 * nz, 16, HD).astype(F32)
+        all_rows = gat[:, :, g].reshape(4 * nz, 16, HD).astype(F32)
         kp[g] = all_rows[:, 0:8].reshape(npr, HD).astype(BF)
         vp[g] = all_rows[:, 8:16].reshape(npr, HD).astype(BF)
         for slot in range(4):
@@ -594,7 +594,7 @@
     resp_out(last)
     prompt_out(last)
 
-    sent = gat.at[0, 0, pl.ds(0, nz - 1)]
+    sent = gat.at[0, 0, pl.ds(0, HK), pl.ds(0, nz - 1)]
     pltpu.make_async_remote_copy(
         src_ref=sent,
         dst_ref=sent,
@@ -670,7 +670,7 @@
         ((HD, flat), BF),
         ((HD, flat), BF),
         ((HK, 4, 2 * HD + 16, HD), BF),
-        ((2, 2, nz, HK, 16, HD), BF),
+        ((2, 2, HK, nz, 16, HD), BF),
         ((4, HD, HD), F32),
         ((quads, 4, HD, 2 * HD), F32),
         ((quads, 4, HD, 2 * HD), F32),

time: 80.5 us -> 80.6 us (level)
  no operation moved by 1% of the time
where the time goes in v7:
time: 80.6 us; the launch traced here: 80.4 us
  Pallas kernels  79.8 us (99%)
    pallas_call x1, Pallas kernels, on_device(): pl.pallas_call(lambda *refs: body(nz, *refs), out_shape=shapes, in_specs=...  77.5 us
    pallas_call x1, Pallas kernels, on_device(): pl.pallas_call(hand_over, out_shape=shapes, in_specs=[whole] * 5, out_spe...  2.23 us

profile of v7, /device:TPU:24, one launch (start us, length us, event | category | flops | bytes accessed | tf_op | source)
XLA Modules:
  0.0 80.4 jit_solution(16143157571365761901)
XLA Ops:
  0.6 77.5 %attention_backward.1 = (bf16[128,4096]{1,0:T(8,128)(2,1)}, f32[128,512]{1,0:T(8,128)}, f32[128,512]{1,0:T(8,128)}, f32[8,512]{1,0:T(8,128)}, f32[8,512]{1,0:T(8,128)}) custom-call(bf16[128,4096]{1,0:T(8,128)(2,1)} %refs_0_.1, bf16[128,512]{1,0:T(8,128)(2,1)} %refs_1_.1, bf16[128,512]{1,0:T(8,128)(2,1)} %refs_2_.1, bf16[8,512]{1,0:T(8,128)(2,1)} %refs_3_.1, ...), custom_call_target="tpu_custom_call" | custom-call | flops 6000000000 | bytes 6000000 | tf_op jit(solution)/shard_map/attention_backward/pallas_call | solution.py:717
  78.2 2.2 %hand_over.1 = (bf16[128,4096]{1,0:T(8,128)(2,1)}, f32[128,512]{1,0:T(8,128)}, f32[128,512]{1,0:T(8,128)}, f32[8,512]{1,0:T(8,128)}, f32[8,512]{1,0:T(8,128)}) custom-call(bf16[128,4096]{1,0:T(8,128)(2,1)} %get-tuple-element.10.refs_0_, f32[128,512]{1,0:T(8,128)} %get-tuple-element.11.refs_1_, f32[128,512]{1,0:T(8,128)} %get-tuple-element.12.refs_2_, ...), custom_call_target="tpu_custom_call" | custom-call | bytes 3000000 | tf_op jit(solution)/shard_map/hand_over/pallas_call | solution.py:750
